TPU v7x, 32 devices: a whole 2x2x4 slice. The times are simulated.
32 devices in a mesh: req: 8 (over z, y), exp: 4 (over x, core).
Axes of the slice: x: 2, y: 2, z: 4, core: 2. Of those that a mesh axis runs over, the one named last changes fastest.
Arguments:
- hidden_in: bfloat16 [2048, 2048], P(('req', 'exp')), may hold values from -6 to 6
- query_in: bfloat16 [2048, 2048], P('req', 'exp'), may hold values from -6 to 6
- key_in: bfloat16 [2048, 2048], P('req', 'exp'), may hold values from -6 to 6
- value_in: bfloat16 [2048, 2048], P('req', 'exp'), may hold values from -24 to 24
- query_gain: float32 [128], replicated, may hold values from 0.5 to 2.5
- key_gain: float32 [128], replicated, may hold values from 0.5 to 2.5
- cache_keys: bfloat16 [16, 32, 2048], P('req', None, 'exp'), may hold values from -400 to 400
- cache_values: bfloat16 [16, 32, 2048], P('req', None, 'exp'), may hold values from -24 to 24
- cache_block: int32 [32], replicated, may hold values from -1 to 15, as said below
- request_lengths: int32 [8, 4], P('req'), may hold values from 1 to 128, 256 in all within a row
- out_proj: bfloat16 [2048, 2048], P('exp'), may hold values from -0.125 to 0.125
- norm_gain: float32 [2048], replicated, may hold values from 0.25 to 1.75
- expert_ids: int32 [2048, 8], P(('req', 'exp')), may hold values from 0 to 15, all different within a row; in each aligned block of 64 rows (0 to 63, 64 to 127, ...) at most 40 rows name the same one
- gate_values: float32 [2048, 8], P(('req', 'exp')), may hold values from 0.4 to 1.6
- old_slots: int32 [16], replicated, may hold values from 0 to 15, each once
- new_replicas: int32 [8], replicated, may hold values from 0 to 15
- slot_weights: bfloat16 [16, 3, 2048, 1024], P('req', None, None, 'exp'), may hold values from -0.125 to 0.125
Outputs:
- layer_out: bfloat16 [2048, 2048], P(('req', 'exp'))
- replica_weights: bfloat16 [8, 3, 2048, 1024], P('req', None, None, 'exp')
Inputs may be any that keep to these rules, and one draw needn't show every extreme that they name: `cache_block`: each index of req has exactly 2 of its 4 requests with a block; every block serves exactly one request. `expert_ids`: in each aligned block of 64 rows (the rows of one device) no expert is named by more than 40 rows, a bound that some block reaches; the 8 experts of a row differ. `old_slots`: every expert is in exactly one slot. `request_lengths`: the lengths of each index of req sum to 256.
All inputs are finite; a program needn't handle non-finite values.
Results may differ from a plain program's by a relative error of at most 0.025.
Values may be sent and summed in bfloat16 or wider, within the bound.
No kernel may reach another device: no remote copies, remote signals or barrier semaphores. Data moves between devices by JAX's collectives and lax.ppermute only.
A program may use at most 128 MiB of HBM per device.

v0:
```python
import math

import jax
import jax.numpy as jnp
from jax import lax
from jax.sharding import PartitionSpec as P


def prepare(values, gain, position):
    vector = values.astype(jnp.float32)
    scaled = vector * lax.rsqrt(jnp.mean(vector * vector, axis=-1, keepdims=True) + 1e-06) * gain
    half_size = scaled.shape[-1] // 2
    frequency = 10000.0 ** (-(jnp.arange(half_size, dtype=jnp.float32) * 2.0 / scaled.shape[-1]))
    angles = position[:, None] * frequency[None, :]
    cosine = jnp.cos(angles)[:, None, :]
    sine_part = jnp.sin(angles)[:, None, :]
    lower_half = scaled[..., :half_size]
    upper_half = scaled[..., half_size:]
    rotated = jnp.concatenate(
        [
            lower_half * cosine - upper_half * sine_part,
            upper_half * cosine + lower_half * sine_part,
        ],
        axis=-1,
    )
    return rotated.astype(jnp.bfloat16)


def compact(block_rows, slots_wanted):
    live = block_rows >= 0
    ranks = jnp.cumsum(live.astype(jnp.int32), axis=1) - 1
    request_idx = jnp.arange(block_rows.shape[1], dtype=jnp.int32)[None, :]
    chosen_blocks = []
    chosen_requests = []
    for slot_num in range(slots_wanted):
        picked = live & (ranks == slot_num)
        chosen_blocks.append(jnp.sum(jnp.where(picked, block_rows, 0), axis=1))
        chosen_requests.append(jnp.sum(jnp.where(picked, request_idx, 0), axis=1))
    return (jnp.stack(chosen_blocks, axis=1), jnp.stack(chosen_requests, axis=1))


def run_slots(inbox, slot_weights, capacity):
    sources = inbox.shape[0]
    model_width = inbox.shape[2]
    slot_count = slot_weights.shape[0]
    grouped = inbox.reshape(sources, slot_count, capacity, model_width)
    results = []
    for slot_num in range(slot_count):
        in_rows = grouped[:, slot_num].reshape(sources * capacity, model_width)
        gate_act = jnp.dot(in_rows, slot_weights[slot_num, 0], preferred_element_type=jnp.float32)
        up_act = jnp.dot(in_rows, slot_weights[slot_num, 1], preferred_element_type=jnp.float32)
        hidden = (jax.nn.silu(gate_act) * up_act).astype(jnp.bfloat16)
        partial_value = lax.dot_general(
            hidden,
            slot_weights[slot_num, 2],
            (((1,), (1,)), ((), ())),
            preferred_element_type=jnp.float32,
        )
        results.append(partial_value.reshape(sources, capacity, model_width))
    return jnp.stack(results, axis=1).reshape(sources, slot_count * capacity, model_width)


def body(
    hidden_in,
    query_in,
    key_in,
    value_in,
    query_gain,
    key_gain,
    cache_keys,
    cache_values,
    cache_block,
    request_lengths,
    out_proj,
    norm_gain,
    expert_ids,
    gate_values,
    old_slots,
    new_replicas,
    slot_weights,
):
    req_count = lax.axis_size("req")
    exp_count = lax.axis_size("exp")
    group_idx = lax.axis_index("req")
    tok_grp, width_q = query_in.shape
    tok_dev, model_width = hidden_in.shape
    head_size = query_gain.shape[0]
    head_count = width_q // head_size
    cache_dev = cache_keys.shape[0]
    pre_len = cache_keys.shape[1]
    req_grp = request_lengths.shape[1]
    lengths = request_lengths[0]
    req_ends = jnp.cumsum(lengths)
    starts = req_ends - lengths
    places = jnp.arange(tok_grp, dtype=jnp.int32)
    member = (places[:, None] >= starts[None, :]) & (places[:, None] < req_ends[None, :])
    request_idx = jnp.arange(req_grp, dtype=jnp.int32)
    segment = jnp.sum(jnp.where(member, request_idx[None, :], 0), axis=1)
    offset = places - jnp.sum(jnp.where(member, starts[None, :], 0), axis=1)
    block_rows = cache_block.reshape(req_count, req_grp)
    my_blocks = lax.dynamic_index_in_dim(block_rows, group_idx, 0, keepdims=False)
    has_cache = my_blocks >= 0
    token_cached = jnp.sum(jnp.where(member & has_cache[None, :], 1, 0), axis=1) > 0
    position = (offset + jnp.where(token_cached, pre_len, 0)).astype(jnp.float32)
    need_blocks, need_requests = compact(block_rows, cache_dev)
    my_requests = lax.dynamic_index_in_dim(need_requests, group_idx, 0, keepdims=False)
    every_keys, every_values = (
        lax.all_gather(cache_keys, "req", axis=0, tiled=True),
        lax.all_gather(cache_values, "req", axis=0, tiled=True),
    )
    wanted = lax.dynamic_index_in_dim(need_blocks, group_idx, 0, keepdims=False)
    far_keys = jnp.take(every_keys, wanted, axis=0)
    far_values = jnp.take(every_values, wanted, axis=0)
    query_n = prepare(query_in.reshape(tok_grp, head_count, head_size), query_gain, position)
    key_n = prepare(key_in.reshape(tok_grp, head_count, head_size), key_gain, position)
    keyset = jnp.concatenate(
        [key_n, far_keys.reshape(cache_dev * pre_len, head_count, head_size)], axis=0
    )
    valueset = jnp.concatenate(
        [
            value_in.reshape(tok_grp, head_count, head_size),
            far_values.reshape(cache_dev * pre_len, head_count, head_size),
        ],
        axis=0,
    )
    key_request = jnp.concatenate([segment, jnp.repeat(my_requests, pre_len)])
    allowed = segment[:, None] == key_request[None, :]
    scores = jnp.einsum("qhd,khd->hqk", query_n, keyset, preferred_element_type=jnp.float32) * (
        1.0 / math.sqrt(head_size)
    )
    scores = jnp.where(allowed[None], scores, -1e30)
    peak = jnp.max(scores, axis=-1, keepdims=True)
    expos = jnp.exp(scores - peak)
    weights = (expos / jnp.sum(expos, axis=-1, keepdims=True)).astype(jnp.bfloat16)
    attended = jnp.einsum("hqk,khd->qhd", weights, valueset, preferred_element_type=jnp.float32)
    attended = attended.astype(jnp.bfloat16).reshape(tok_grp, width_q)
    attn_out = lax.psum_scatter(
        jnp.dot(attended, out_proj, preferred_element_type=jnp.float32),
        "exp",
        scatter_dimension=0,
        tiled=True,
    )
    residual = hidden_in.astype(jnp.float32) + attn_out
    normed = (
        residual
        * lax.rsqrt(jnp.mean(residual * residual, axis=-1, keepdims=True) + 1e-06)
        * norm_gain
    ).astype(jnp.bfloat16)
    topk_count = expert_ids.shape[1]
    slot_total = old_slots.shape[0]
    slots_here = slot_weights.shape[0]
    capacity = max(2, tok_dev * topk_count * 5 // (4 * slot_total))
    slot_range = jnp.arange(slot_total, dtype=jnp.int32)
    slot_of = jnp.sum(
        jnp.where(old_slots[None, :] == slot_range[:, None], slot_range[None, :], 0), axis=1
    )
    flat_ids = expert_ids.reshape(-1)
    onehot = flat_ids[:, None] == slot_range[None, :]
    row_slot = jnp.sum(jnp.where(onehot, slot_of[None, :], 0), axis=1)
    before = jnp.cumsum(onehot.astype(jnp.int32), axis=0) - onehot.astype(jnp.int32)
    row_rank = jnp.sum(jnp.where(onehot, before, 0), axis=1)
    target = row_slot * capacity + row_rank
    send_rows = jnp.repeat(normed, topk_count, axis=0)
    outbox = jnp.zeros((slot_total * capacity, model_width), jnp.bfloat16).at[target].set(send_rows)
    outbox = outbox.reshape(req_count, slots_here * capacity, model_width)
    copies = jnp.broadcast_to(
        outbox[:, None], (req_count, exp_count, slots_here * capacity, model_width)
    )
    copies = copies.reshape(req_count * exp_count, slots_here * capacity, model_width)
    inbox = lax.all_to_all(copies, ("req", "exp"), split_axis=0, concat_axis=0, tiled=True)
    partial_value = run_slots(inbox, slot_weights, capacity).astype(jnp.bfloat16)
    returned = lax.all_to_all(
        partial_value, ("req", "exp"), split_axis=0, concat_axis=0, tiled=True
    )
    result = jnp.sum(
        returned.astype(jnp.float32).reshape(
            req_count, exp_count, slots_here * capacity, model_width
        ),
        axis=1,
    )
    result_rows = jnp.take(result.reshape(slot_total * capacity, model_width), target, axis=0)
    mixture = jnp.sum(
        result_rows.reshape(tok_dev, topk_count, model_width) * gate_values[:, :, None], axis=1
    )
    layer_out = (residual + mixture).astype(jnp.bfloat16)
    spread_slots = lax.all_to_all(slot_weights, "req", split_axis=2, concat_axis=0, tiled=True)
    replica_onehot = new_replicas[:, None] == slot_range[None, :]
    source_slot = jnp.sum(jnp.where(replica_onehot, slot_of[None, :], 0), axis=1)
    chosen_pieces = jnp.take(spread_slots, source_slot, axis=0)
    replica_weights = lax.all_to_all(chosen_pieces, "req", split_axis=0, concat_axis=2, tiled=True)
    return (layer_out, replica_weights)


def solution(mesh):
    in_specs = (
        P(("req", "exp"), None),
        P("req", "exp"),
        P("req", "exp"),
        P("req", "exp"),
        P(),
        P(),
        P("req", None, "exp"),
        P("req", None, "exp"),
        P(),
        P("req", None),
        P("exp", None),
        P(),
        P(("req", "exp"), None),
        P(("req", "exp"), None),
        P(),
        P(),
        P("req", None, None, "exp"),
    )
    out_specs = (P(("req", "exp"), None), P("req", None, None, "exp"))
    return jax.shard_map(body, mesh=mesh, in_specs=in_specs, out_specs=out_specs, check_vma=False)
```

profile of v0, /device:TPU:0, one launch (start us, length us, event | category | flops | bytes accessed | tf_op | source)
XLA Modules:
  0.0 899.8 jit_solution(8354215778483193846)
XLA Ops:
  7.2 10.6 %copy.78 = bf16[2,3,2048,256]{3,1,0,2:T(4,128)(2,1)} copy(bf16[2,3,2048,256]{3,2,1,0:T(8,128)(2,1)} %param.35) | data formatting | bytes 12582912 | tf_op args[16]
  17.8 7.4 all-to-all-start.2
  26.0 203.5 %all_gather.6 = bf16[16,32,512]{2,1,0:T(8,128)(2,1)S(1)} all-gather(bf16[2,32,512]{2,1,0:T(8,128)(2,1)S(1)} %copy-done.7), channel_id=1, replica_groups=mesh['req'=8,'exp'=4] {'req'}, dimensions={0}, use_global_device_ids=true | all-gather | bytes 589824 | tf_op jit(solution)/shard_map/all_gather | solution.py:109
  229.5 0.6 gather_fusion.2
  230.1 31.3 %all_gather.7 = bf16[16,32,512]{2,1,0:T(8,128)(2,1)S(1)} all-gather(bf16[2,32,512]{2,1,0:T(8,128)(2,1)S(1)} %copy-done.8), channel_id=1, replica_groups=mesh['req'=8,'exp'=4] {'req'}, dimensions={0}, use_global_device_ids=true | all-gather | bytes 589824 | tf_op jit(solution)/shard_map/all_gather | solution.py:108
  261.4 0.6 gather_fusion.3
  263.1 0.9 copy.71
  264.0 0.6 copy.67
  264.7 1.1 copy.65
  265.8 0.8 copy.66
  266.6 0.7 fusion.49
  267.7 0.5 multiply_cosine_fusion
  268.2 1.4 multiply_multiply_fusion
  269.7 0.4 subtract_convert_fusion.1
  270.1 2.3 fusion.63
  272.5 1.7 convolution_convert_fusion
  274.2 2.0 fusion.68
  276.6 1.2 reduce-window.11
  277.8 0.2 slice_reduce_fusion
  278.3 28.9 %reduce-scatter.2.cloned.1.call-done = f32[64,2048]{1,0:T(8,128)} async-done(((f32[256,2048]{1,0:T(8,128)}), f32[64,2048]{1,0:T(8,128)}) %reduce-scatter.2.cloned.1.call-update) | async-done | bytes 524304 | tf_op jit(solution)/shard_map/reduce_scatter | solution.py:137
  307.2 1.2 multiply_reduce_fusion
  308.5 1.2 multiply_convert_fusion
  309.6 5.4 scatter_custom_fusion
  315.0 7.0 broadcast_in_dim.196
  322.0 4.7 all-to-all-start
  327.0 4.9 copy.79
  331.9 3.1 copy.80
  335.0 5.2 gather_fusion.1
  340.2 3.9 broadcast_select_fusion
  344.1 214.9 %all-to-all-done = bf16[32,80,2048]{2,1,0:T(8,128)(2,1)} async-done(((bf16[32,80,2048]{2,1,0:T(8,128)(2,1)}), bf16[32,80,2048]{2,1,0:T(8,128)(2,1)}, u32[]{:S(2)}, u32[]{:S(2)}) %all-to-all-start) | async-done | bytes 10485792 | tf_op jit(solution)/shard_map/all_to_all | solution.py:170
  559.0 4.5 all-to-all-start.3
  563.5 10.2 %fusion.62 = (bf16[32,1,40,2048]{3,2,1,0:T(8,128)(2,1)}, bf16[32,1,40,2048]{3,2,1,0:T(8,128)(2,1)}) fusion(bf16[32,2,40,2048]{3,2,1,0:T(8,128)(2,1)} %bitcast.22), kind=kLoop, calls=%fused_computation.133 | loop fusion | bytes 20971520 | tf_op jit(solution)/shard_map/slice | solution.py:49
  573.7 4.5 fusion.17
  578.2 4.6 fusion.3
  582.9 3.8 convert_bitcast_fusion.1
  586.7 1.6 fusion.14
  588.3 1.7 fusion.4
  590.0 3.9 convert_bitcast_fusion
  594.0 9.0 %pad_maximum_fusion = bf16[32,2,40,2048]{3,2,0,1:T(8,128)(2,1)} fusion(bf16[32,1,40,2048]{3,2,0,1:T(8,128)(2,1)} %convert_bitcast_fusion, bf16[32,1,40,2048]{3,2,0,1:T(8,128)(2,1)} %convert_bitcast_fusion.1), kind=kLoop, calls=%fused_computation.7 | loop fusion | flops 5242880 | bytes 20971520 | tf_op jit(solution)/shard_map/stack | solution.py:60
  603.0 10.2 %copy.76 = bf16[32,2,40,2048]{3,2,1,0:T(8,128)(2,1)} copy(bf16[32,2,40,2048]{3,2,0,1:T(8,128)(2,1)} %pad_maximum_fusion) | data formatting | bytes 20971520 | tf_op jit(solution)/shard_map/stack | solution.py:60
  613.2 21.1 %all-to-all-done.3 = bf16[8,3,256,256]{3,2,1,0:T(8,128)(2,1)} async-done(((bf16[8,3,256,256]{3,2,1,0:T(8,128)(2,1)}), bf16[8,3,256,256]{3,2,1,0:T(8,128)(2,1)}, u32[]{:S(2)}, u32[]{:S(2)}) %all-to-all-start.3) | async-done | bytes 3145760 | tf_op jit(solution)/shard_map/all_to_all | solution.py:190
  634.3 3.8 all-to-all-start.1
  638.3 3.9 copy.81
  642.2 228.4 %all-to-all-done.1 = bf16[32,80,2048]{2,1,0:T(8,128)(2,1)} async-done(((bf16[32,80,2048]{2,1,0:T(8,128)(2,1)}), bf16[32,80,2048]{2,1,0:T(8,128)(2,1)}, u32[]{:S(2)}, u32[]{:S(2)}) %all-to-all-start.1) | async-done | bytes 10485792 | tf_op jit(solution)/shard_map/all_to_all | solution.py:172
  870.6 9.5 %convert_reduce_fusion = f32[8,80,2048]{2,1,0:T(8,128)} fusion(bf16[32,80,2048]{2,1,0:T(8,128)(2,1)} %all-to-all-done.1), kind=kLoop, calls=%fused_computation.6 | loop fusion | flops 9175040 | bytes 15728640 | tf_op jit(solution)/shard_map/reduce_sum | solution.py:175
  880.1 8.0 gather_fusion
  888.1 4.1 fusion.2
  892.2 0.8 add_convert_fusion
  (96 shorter events, 3.2 us)
Async XLA Ops:
  7.2 267.1 %copy-start = (bf16[512,2048]{1,0:T(8,128)(2,1)S(1)}, bf16[512,2048]{1,0:T(8,128)(2,1)}, u32[]{:S(2)}) copy-start(bf16[512,2048]{1,0:T(8,128)(2,1)} %param.29) | copy-start | bytes 6291460
  17.8 7.5 copy-start.12
  17.8 8.2 copy-start.7
  17.8 212.3 %copy-start.8 = (bf16[2,32,512]{2,1,0:T(8,128)(2,1)S(1)}, bf16[2,32,512]{2,1,0:T(8,128)(2,1)}, u32[]{:S(2)}) copy-start(bf16[2,32,512]{2,1,0:T(8,128)(2,1)} %param.25) | copy-start | bytes 196612
  17.8 244.7 %copy-start.13 = (s32[1,4]{1,0:T(1,128)S(1)}, s32[1,4]{1,0:T(1,128)}, u32[]{:S(2)}) copy-start(s32[1,4]{1,0:T(1,128)} %param.28) | copy-start | bytes 52
  17.8 244.8 %copy-start.4 = (bf16[256,512]{1,0:T(8,128)(2,1)S(1)}, bf16[256,512]{1,0:T(8,128)(2,1)}, u32[]{:S(2)}) copy-start(bf16[256,512]{1,0:T(8,128)(2,1)} %param.20) | copy-start | bytes 786436
  17.8 245.1 %copy-start.5 = (bf16[256,512]{1,0:T(8,128)(2,1)S(1)}, bf16[256,512]{1,0:T(8,128)(2,1)}, u32[]{:S(2)}) copy-start(bf16[256,512]{1,0:T(8,128)(2,1)} %param.21) | copy-start | bytes 786436
  17.8 297.2 %all-to-all-start.2 = ((bf16[2,3,2048,256]{3,1,0,2:T(4,128)(2,1)}), bf16[2,3,2048,256]{3,1,0,2:T(4,128)(2,1)}, u32[]{:S(2)}, u32[]{:S(2)}) async-start(bf16[2,3,2048,256]{3,1,0,2:T(4,128)(2,1)} %copy.78), calls=%async_computation.3 | async-start | bytes 16777216 | tf_op jit(solution)/shard_map/all_to_all | solution.py:186
  25.3 282.0 %reduce-scatter.2.cloned.1.call-start = ((), (), s32[]{:S(2)}) async-start(), calls=%async_computation.5 | async-start | bytes 2621440 | tf_op jit(solution)/shard_map/reduce_scatter | solution.py:137
  268.2 4.3 copy-start.6
  274.2 2.1 copy-start.10
  274.2 3.8 copy-start.14
  274.2 33.0 %copy-start.3 = (bf16[64,2048]{1,0:T(8,128)(2,1)S(1)}, bf16[64,2048]{1,0:T(8,128)(2,1)}, u32[]{:S(2)}) copy-start(bf16[64,2048]{1,0:T(8,128)(2,1)} %param.19) | copy-start | bytes 786436
  274.2 34.2 %copy-start.9 = (f32[2048]{0:T(1024)S(1)}, f32[2048]{0:T(1024)}, u32[]{:S(2)}) copy-start(f32[2048]{0:T(1024)} %param.30) | copy-start | bytes 24580
  322.0 4.7 copy-start.15
  322.0 237.0 %all-to-all-start = ((bf16[32,80,2048]{2,1,0:T(8,128)(2,1)}), bf16[32,80,2048]{2,1,0:T(8,128)(2,1)}, u32[]{:S(2)}, u32[]{:S(2)}) async-start(bf16[32,80,2048]{2,1,0:T(8,128)(2,1)} %bitcast.113), calls=%async_computation.1 | async-start | bytes 20971520 | tf_op jit(solution)/shard_map/all_to_all | solution.py:170
  559.0 75.2 %all-to-all-start.3 = ((bf16[8,3,256,256]{3,2,1,0:T(8,128)(2,1)}), bf16[8,3,256,256]{3,2,1,0:T(8,128)(2,1)}, u32[]{:S(2)}, u32[]{:S(2)}) async-start(bf16[8,3,256,256]{3,2,1,0:T(8,128)(2,1)} %broadcast_select_fusion), calls=%async_computation.4 | async-start | bytes 6291456 | tf_op jit(solution)/shard_map/all_to_all | solution.py:190
  573.7 9.2 %slice-start = ((s8[6291456]{0:T(1024)(128)(4,1)}), s8[4194304]{0:T(1024)(128)(4,1)S(1)}, s32[]{:S(2)}) async-start(s8[6291456]{0:T(1024)(128)(4,1)} %bitcast.117), calls=%async_computation.6 | async-start | bytes 8388608
  573.7 13.0 %slice-start.2 = ((s8[5242880]{0:T(1024)(128)(4,1)}), s8[4194304]{0:T(1024)(128)(4,1)S(1)}, s32[]{:S(2)}) async-start(s8[5242880]{0:T(1024)(128)(4,1)} %bitcast.120), calls=%async_computation.8 | async-start | bytes 8388608
  578.2 4.7 slice-start.1
  578.2 8.5 slice-start.3
  634.3 3.9 copy-start.11
  634.3 236.3 %all-to-all-start.1 = ((bf16[32,80,2048]{2,1,0:T(8,128)(2,1)}), bf16[32,80,2048]{2,1,0:T(8,128)(2,1)}, u32[]{:S(2)}, u32[]{:S(2)}) async-start(bf16[32,80,2048]{2,1,0:T(8,128)(2,1)} %bitcast.114), calls=%async_computation.2 | async-start | bytes 20971520 | tf_op jit(solution)/shard_map/all_to_all | solution.py:172
  880.1 12.9 %copy-start.1 = (bf16[512,2048]{1,0:T(8,128)(2,1)S(1)}, bf16[512,2048]{1,0:T(8,128)(2,1)}, u32[]{:S(2)}) copy-start(bf16[512,2048]{1,0:T(8,128)(2,1)} %param.29) | copy-start | bytes 6291460
  888.1 4.1 copy-start.2
Sparse Core Ops, SparseCore 0:
  276.4 30.7 reduce-scatter.1
where the time goes:
time: 901 us; the launch traced here: 900 us
  waiting for transfers between devices  493 us (55%)
  blocking collectives  235 us (26%)
  local copies, waits for them, and re-layouts  74.9 us (8%)
  other arithmetic  35.4 us (4%)
  matrix products  26.3 us (3%)
  starting transfers between devices  20.5 us (2%)
  between operations  14.5 us (2%)
    all_to_all x1, waiting for transfers between devices, body(): lax.all_to_all(partial_value, ('req', 'exp'), split_axis=0, concat_axis=0...  228 us
    all_to_all x1, waiting for transfers between devices, body(): lax.all_to_all(copies, ('req', 'exp'), split_axis=0, concat_axis=0, tiled...  215 us
    all_gather x1, blocking collectives, body(): lax.all_gather(cache_values, 'req', axis=0, tiled=True)  204 us
    all_gather x1, blocking collectives, body(): lax.all_gather(cache_keys, 'req', axis=0, tiled=True)  31.3 us
    reduce_scatter x1, waiting for transfers between devices, body(): lax.psum_scatter(jnp.dot(attended, out_proj, preferred_element_type=jnp.f...  28.9 us
    all_to_all x1, waiting for transfers between devices, body(): lax.all_to_all(chosen_pieces, 'req', split_axis=0, concat_axis=2, tiled=T...  21.1 us
  transfers between devices with their start and end apart: 5, of which 4 were waited for; matrix products, arithmetic and copies ran while one was open for 11% of the time, Pallas kernels for 0%

commit v1 on v0

--- a/solution.py
+++ b/solution.py
@@ -3,6 +3,8 @@
 import jax
 import jax.numpy as jnp
 from jax import lax
+from jax.experimental import pallas as pl
+from jax.experimental.pallas import tpu as pltpu
 from jax.sharding import PartitionSpec as P
 
 
@@ -39,25 +41,46 @@
     return (jnp.stack(chosen_blocks, axis=1), jnp.stack(chosen_requests, axis=1))
 
 
-def run_slots(inbox, slot_weights, capacity):
-    sources = inbox.shape[0]
-    model_width = inbox.shape[2]
-    slot_count = slot_weights.shape[0]
-    grouped = inbox.reshape(sources, slot_count, capacity, model_width)
-    results = []
+def experts_kernel(tok_ref, gate_ref, weights_ref, out_ref):
+    rows = tok_ref[...]
+    slot_count = weights_ref.shape[0]
+    total = None
     for slot_num in range(slot_count):
-        in_rows = grouped[:, slot_num].reshape(sources * capacity, model_width)
-        gate_act = jnp.dot(in_rows, slot_weights[slot_num, 0], preferred_element_type=jnp.float32)
-        up_act = jnp.dot(in_rows, slot_weights[slot_num, 1], preferred_element_type=jnp.float32)
-        hidden = (jax.nn.silu(gate_act) * up_act).astype(jnp.bfloat16)
-        partial_value = lax.dot_general(
+        gate_act = jnp.dot(rows, weights_ref[slot_num, 0], preferred_element_type=jnp.float32)
+        up_act = jnp.dot(rows, weights_ref[slot_num, 1], preferred_element_type=jnp.float32)
+        factor = gate_ref[:, slot_num : slot_num + 1]
+        hidden = gate_act / (1.0 + jnp.exp(-gate_act)) * up_act
+        hidden = (hidden * factor).astype(jnp.bfloat16)
+        part = lax.dot_general(
             hidden,
-            slot_weights[slot_num, 2],
+            weights_ref[slot_num, 2],
             (((1,), (1,)), ((), ())),
             preferred_element_type=jnp.float32,
         )
-        results.append(partial_value.reshape(sources, capacity, model_width))
-    return jnp.stack(results, axis=1).reshape(sources, slot_count * capacity, model_width)
+        total = part if total is None else total + part
+    out_ref[...] = total.astype(out_ref.dtype)
+
+
+def run_experts(tokens, gates, slot_weights, block):
+    count, width = tokens.shape
+    slots_here, mats, _, hidden_size = slot_weights.shape
+    return pl.pallas_call(
+        experts_kernel,
+        out_shape=jax.ShapeDtypeStruct((count, width), jnp.bfloat16),
+        grid=(count // block,),
+        in_specs=[
+            pl.BlockSpec((block, width), lambda i: (i, 0)),
+            pl.BlockSpec((block, slots_here), lambda i: (i, 0)),
+            pl.BlockSpec((slots_here, mats, width, hidden_size), lambda i: (0, 0, 0, 0)),
+        ],
+        out_specs=pl.BlockSpec((block, width), lambda i: (i, 0)),
+        compiler_params=pltpu.CompilerParams(vmem_limit_bytes=40 * 1024 * 1024),
+        cost_estimate=pl.CostEstimate(
+            flops=2 * count * width * hidden_size * mats * slots_here,
+            bytes_accessed=4 * count * width + 2 * slot_weights.size,
+            transcendentals=count * hidden_size * slots_here,
+        ),
+    )(tokens, gates, slot_weights)
 
 
 def body(
@@ -104,13 +127,10 @@
     position = (offset + jnp.where(token_cached, pre_len, 0)).astype(jnp.float32)
     need_blocks, need_requests = compact(block_rows, cache_dev)
     my_requests = lax.dynamic_index_in_dim(need_requests, group_idx, 0, keepdims=False)
-    every_keys, every_values = (
-        lax.all_gather(cache_keys, "req", axis=0, tiled=True),
-        lax.all_gather(cache_values, "req", axis=0, tiled=True),
-    )
+    every_cache = lax.all_gather(jnp.stack([cache_keys, cache_values]), "req", axis=1, tiled=True)
     wanted = lax.dynamic_index_in_dim(need_blocks, group_idx, 0, keepdims=False)
-    far_keys = jnp.take(every_keys, wanted, axis=0)
-    far_values = jnp.take(every_values, wanted, axis=0)
+    far_cache = jnp.take(every_cache, wanted, axis=1)
+    far_keys, far_values = far_cache[0], far_cache[1]
     query_n = prepare(query_in.reshape(tok_grp, head_count, head_size), query_gain, position)
     key_n = prepare(key_in.reshape(tok_grp, head_count, head_size), key_gain, position)
     keyset = jnp.concatenate(
@@ -146,43 +166,22 @@
         * lax.rsqrt(jnp.mean(residual * residual, axis=-1, keepdims=True) + 1e-06)
         * norm_gain
     ).astype(jnp.bfloat16)
-    topk_count = expert_ids.shape[1]
     slot_total = old_slots.shape[0]
     slots_here = slot_weights.shape[0]
-    capacity = max(2, tok_dev * topk_count * 5 // (4 * slot_total))
     slot_range = jnp.arange(slot_total, dtype=jnp.int32)
     slot_of = jnp.sum(
         jnp.where(old_slots[None, :] == slot_range[:, None], slot_range[None, :], 0), axis=1
     )
-    flat_ids = expert_ids.reshape(-1)
-    onehot = flat_ids[:, None] == slot_range[None, :]
-    row_slot = jnp.sum(jnp.where(onehot, slot_of[None, :], 0), axis=1)
-    before = jnp.cumsum(onehot.astype(jnp.int32), axis=0) - onehot.astype(jnp.int32)
-    row_rank = jnp.sum(jnp.where(onehot, before, 0), axis=1)
-    target = row_slot * capacity + row_rank
-    send_rows = jnp.repeat(normed, topk_count, axis=0)
-    outbox = jnp.zeros((slot_total * capacity, model_width), jnp.bfloat16).at[target].set(send_rows)
-    outbox = outbox.reshape(req_count, slots_here * capacity, model_width)
-    copies = jnp.broadcast_to(
-        outbox[:, None], (req_count, exp_count, slots_here * capacity, model_width)
-    )
-    copies = copies.reshape(req_count * exp_count, slots_here * capacity, model_width)
-    inbox = lax.all_to_all(copies, ("req", "exp"), split_axis=0, concat_axis=0, tiled=True)
-    partial_value = run_slots(inbox, slot_weights, capacity).astype(jnp.bfloat16)
-    returned = lax.all_to_all(
-        partial_value, ("req", "exp"), split_axis=0, concat_axis=0, tiled=True
-    )
-    result = jnp.sum(
-        returned.astype(jnp.float32).reshape(
-            req_count, exp_count, slots_here * capacity, model_width
-        ),
+    dense_gates = jnp.sum(
+        jnp.where(expert_ids[:, :, None] == old_slots[None, None, :], gate_values[:, :, None], 0.0),
         axis=1,
     )
-    result_rows = jnp.take(result.reshape(slot_total * capacity, model_width), target, axis=0)
-    mixture = jnp.sum(
-        result_rows.reshape(tok_dev, topk_count, model_width) * gate_values[:, :, None], axis=1
-    )
-    layer_out = (residual + mixture).astype(jnp.bfloat16)
+    every_gates = lax.all_gather(dense_gates, ("req", "exp"), axis=0, tiled=True)
+    my_gates = lax.dynamic_slice_in_dim(every_gates, group_idx * slots_here, slots_here, axis=1)
+    tokens = lax.all_gather(normed, ("req", "exp"), axis=0, tiled=True)
+    mixed = run_experts(tokens, my_gates, slot_weights, tok_grp)
+    mixture = lax.psum_scatter(mixed, ("req", "exp"), scatter_dimension=0, tiled=True)
+    layer_out = (residual + mixture.astype(jnp.float32)).astype(jnp.bfloat16)
     spread_slots = lax.all_to_all(slot_weights, "req", split_axis=2, concat_axis=0, tiled=True)
     replica_onehot = new_replicas[:, None] == slot_range[None, :]
     source_slot = jnp.sum(jnp.where(replica_onehot, slot_of[None, :], 0), axis=1)

time: 901 us -> 545 us (0.60)
  waiting for transfers between devices: 493 us -> 115 us
  blocking collectives: 235 us -> 335 us
  local copies, waits for them, and re-layouts: 74.9 us -> 36.4 us
  other arithmetic: 35.4 us -> 14.6 us
  matrix products: 26.3 us -> 6.42 us
  Pallas kernels: 0 us -> 17.5 us
  starting transfers between devices: 20.5 us -> 5.83 us
    all_to_all x3 -> x0, waiting for transfers between devices: 464 us -> none  [the longest x1 228 us: body(): lax.all_to_all(partial_value, ('req', 'exp'), split_axis=0, concat_axis=0...]
    all_to_all x0 -> x1, blocking collectives: none -> 130 us  [body(): lax.all_to_all(chosen_pieces, 'req', split_axis=0, concat_axis=2, tiled=T...]
    reduce_scatter x0 -> x1, waiting for transfers between devices: none -> 50.4 us  [body(): lax.psum_scatter(mixed, ('req', 'exp'), scatter_dimension=0, tiled=True)]
    all_gather x0 -> x2, waiting for transfers between devices: none -> 33.9 us  [the longest x1 33.8 us: body(): lax.all_gather(jnp.stack([cache_keys, cache_values]), 'req', axis=1, tile...]
    all_gather x2 -> x1, blocking collectives: 235 us -> 205 us  [body(): lax.all_gather(dense_gates, ('req', 'exp'), axis=0, tiled=True)]
    dot_general x6 -> x0, matrix products: 20.2 us -> none  [the longest x2 7.76 us: run_slots(): lax.dot_general(hidden, slot_weights[slot_num, 2], (((1,), (1,)), ((), ()...]
    pallas_call x0 -> x1, Pallas kernels: none -> 17.5 us  [run_experts(): pl.pallas_call(experts_kernel, out_shape=jax.ShapeDtypeStruct((count, wid...]
    reduce_sum x3 -> x1, other arithmetic: 13.7 us -> 0.08 us  [body(): jnp.sum(jnp.where(expert_ids[:, :, None] == old_slots[None, None, :], gat...]
  transfers between devices with their start and end apart: 5 -> 5, of which waited for: 4 -> 3; matrix products, arithmetic and copies ran while one was open for 11% -> 7% of each run, Pallas kernels for 0% -> 3%
where the time goes in v1:
time: 545 us; the launch traced here: 544 us
  blocking collectives  335 us (61%)
  waiting for transfers between devices  115 us (21%)
  local copies, waits for them, and re-layouts  36.4 us (7%)
  Pallas kernels  17.5 us (3%)
  other arithmetic  14.6 us (3%)
  between operations  14.1 us (3%)
  matrix products  6.42 us (1%)
  starting transfers between devices  5.83 us (1%)
    all_gather x1, blocking collectives, body(): lax.all_gather(dense_gates, ('req', 'exp'), axis=0, tiled=True)  205 us
    all_to_all x1, blocking collectives, body(): lax.all_to_all(chosen_pieces, 'req', split_axis=0, concat_axis=2, tiled=T...  130 us
    reduce_scatter x1, waiting for transfers between devices, body(): lax.psum_scatter(mixed, ('req', 'exp'), scatter_dimension=0, tiled=True)  50.4 us
    all_gather x1, waiting for transfers between devices, body(): lax.all_gather(jnp.stack([cache_keys, cache_values]), 'req', axis=1, tile...  33.8 us
    reduce_scatter x1, waiting for transfers between devices, body(): lax.psum_scatter(jnp.dot(attended, out_proj, preferred_element_type=jnp.f...  30.3 us
    pallas_call x1, Pallas kernels, run_experts(): pl.pallas_call(experts_kernel, out_shape=jax.ShapeDtypeStruct((count, wid...  17.5 us
    unnamed x30, local copies, waits for them, and re-layouts  16.1 us
  transfers between devices with their start and end apart: 5, of which 3 were waited for; matrix products, arithmetic and copies ran while one was open for 7% of the time, Pallas kernels for 3%

profile of v1, /device:TPU:0, one launch (start us, length us, event | category | flops | bytes accessed | tf_op | source)
XLA Modules:
  0.0 544.2 jit_solution(5471796201962091222)
XLA Ops:
  7.2 1.7 pad_maximum_fusion
  9.0 0.7 reshape.212
  9.8 0.2 reduce_window_sum.18
  9.9 0.2 select_reduce_fusion.9
  10.1 0.2 dynamic-slice_reduce_fusion.1
  10.4 0.2 dynamic-slice_reduce_fusion
  10.6 0.1 reshape.215
  10.7 0.8 reduce-window.4
  11.5 0.7 fusion.24
  12.2 1.1 copy.63
  13.4 0.1 select_reduce_fusion.4
  13.5 1.1 copy.61
  14.6 0.1 copy.62
  14.7 0.9 copy.64
  15.7 0.1 copy.58
  15.8 0.2 copy.59
  16.1 0.1 broadcast_compare_fusion
  16.2 0.5 multiply_cosine_fusion
  16.8 1.4 multiply_multiply_fusion
  18.1 1.1 subtract_convert_fusion.1
  19.3 33.8 %all-gather.4.cloned.1.call-done = bf16[2,16,32,512]{3,2,1,0:T(8,128)(2,1)} async-done(((bf16[2,2,32,512]{3,2,1,0:T(8,128)(2,1)}), bf16[2,16,32,512]{3,2,1,0:T(8,128)(2,1)}) %all-gather.4.cloned.1.call-update) | async-done | bytes 1048592 | tf_op jit(solution)/shard_map/all_gather | solution.py:130
  53.1 1.8 gather_fusion
  54.9 0.1 select_bitcast_fusion
  55.1 2.7 fusion.38
  57.8 1.7 convolution_convert_fusion
  59.5 2.1 fusion.43
  61.6 30.3 %reduce-scatter.3.cloned.1.call-done = f32[64,2048]{1,0:T(8,128)} async-done(((f32[256,2048]{1,0:T(8,128)}), f32[64,2048]{1,0:T(8,128)}) %reduce-scatter.3.cloned.1.call-update) | async-done | bytes 524304 | tf_op jit(solution)/shard_map/reduce_scatter | solution.py:157
  91.9 1.2 multiply_reduce_fusion
  93.1 1.9 multiply_convert_fusion
  95.0 10.5 %copy.67 = bf16[2,3,2048,256]{3,1,0,2:T(4,128)(2,1)} copy(bf16[2,3,2048,256]{3,2,1,0:T(8,128)(2,1)} %weights_ref.1) | data formatting | bytes 12582912 | tf_op args[16]
  105.5 5.7 %all-to-all-start = ((bf16[2,3,2048,256]{3,1,0,2:T(4,128)(2,1)}), bf16[2,3,2048,256]{3,1,0,2:T(4,128)(2,1)}, u32[]{:S(2)}, u32[]{:S(2)}) async-start(bf16[2,3,2048,256]{3,1,0,2:T(4,128)(2,1)} %copy.67), calls=%async_computation.2 | async-start | bytes 16777216 | tf_op jit(solution)/shard_map/all_to_all | solution.py:185
  111.2 0.1 select_reduce_fusion
  111.3 204.9 %all-gather = f32[32,64,16]{1,2,0:T(8,128)S(1)} all-gather(f32[1,64,16]{1,2,0:T(8,128)S(1)} %bitcast.67), channel_id=1, replica_groups=mesh['req'=8,'exp'=4] {'req','exp'}, dimensions={0}, use_global_device_ids=true | all-gather | bytes 135168 | tf_op jit(solution)/shard_map/all_gather | solution.py:179
  316.2 0.3 copy.66
  316.5 0.3 constant_dynamic-slice_fusion.gate_ref
  316.9 2.8 copy-done.2
  319.7 17.5 %shard_map.176 = bf16[2048,2048]{1,0:T(8,128)(2,1)} custom-call(bf16[2048,2048]{1,0:T(8,128)(2,1)} %all-gather.6.cloned.1.call-done.tok_ref, f32[2048,2]{1,0:T(8,128)S(1)} %constant_dynamic-slice_fusion.gate_ref, bf16[2,3,2048,256]{3,2,1,0:T(8,128)(2,1)S(1)} %copy-done.2), custom_call_target="tpu_custom_call" | custom-call | flops 12884901888 | bytes 23068672 | tf_op jit(solution)/shard_map/pallas_call | solution.py:67
  337.3 0.1 select_reduce_fusion.1
  337.4 0.5 copy-done.12
  337.9 0.2 select_reduce_fusion.2
  338.1 4.9 copy.68
  343.1 3.1 copy.69
  346.2 5.2 gather_fusion.1
  351.4 2.3 broadcast_select_fusion
  353.6 129.9 %all_to_all.36 = bf16[8,3,256,256]{3,2,1,0:T(8,128)(2,1)S(1)} all-to-all(bf16[8,3,256,256]{3,2,1,0:T(8,128)(2,1)S(1)} %broadcast_select_fusion), channel_id=1, replica_groups=mesh['req'=8,'exp'=4] {'req'}, dimensions={0} | all-to-all | bytes 6291456 | tf_op jit(solution)/shard_map/all_to_all | solution.py:189
  483.5 2.0 copy.70
  485.5 50.4 %reduce-scatter.5.cloned.1.call-done = bf16[64,2048]{1,0:T(8,128)(2,1)} async-done(((bf16[2048,2048]{1,0:T(8,128)(2,1)}), bf16[64,2048]{1,0:T(8,128)(2,1)}) %reduce-scatter.5.cloned.1.call-update) | async-done | bytes 262160 | tf_op jit(solution)/shard_map/reduce_scatter | solution.py:183
  535.9 1.7 add_convert_fusion
  (59 shorter events, 0.7 us)
Async XLA Ops:
  7.2 52.3 %copy-start = (bf16[512,2048]{1,0:T(8,128)(2,1)S(1)}, bf16[512,2048]{1,0:T(8,128)(2,1)}, u32[]{:S(2)}) copy-start(bf16[512,2048]{1,0:T(8,128)(2,1)} %param.27) | copy-start | bytes 6291460
  7.2 8.5 %copy-start.5 = (bf16[256,512]{1,0:T(8,128)(2,1)S(1)}, bf16[256,512]{1,0:T(8,128)(2,1)}, u32[]{:S(2)}) copy-start(bf16[256,512]{1,0:T(8,128)(2,1)} %param.20) | copy-start | bytes 786436
  7.2 45.9 %all-gather.4.cloned.1.call-start = ((), (), s32[]{:S(2)}) async-start(), calls=%async_computation.4 | async-start | bytes 1179648 | tf_op jit(solution)/shard_map/all_gather | solution.py:130
  9.0 82.9 %reduce-scatter.3.cloned.1.call-start = ((), (), s32[]{:S(2)}) async-start(), calls=%async_computation.5 | async-start | bytes 2621440 | tf_op jit(solution)/shard_map/reduce_scatter | solution.py:157
  13.3 3.5 copy-start.10
  13.3 3.5 copy-start.11
  61.6 30.3 %copy-start.4 = (bf16[64,2048]{1,0:T(8,128)(2,1)S(1)}, bf16[64,2048]{1,0:T(8,128)(2,1)}, u32[]{:S(2)}) copy-start(bf16[64,2048]{1,0:T(8,128)(2,1)} %param.17) | copy-start | bytes 786436
  61.6 31.6 %copy-start.6 = (f32[2048]{0:T(1024)S(1)}, f32[2048]{0:T(1024)}, u32[]{:S(2)}) copy-start(f32[2048]{0:T(1024)} %param.28) | copy-start | bytes 24580
  61.6 255.3 %all-gather.6.cloned.1.call-start = ((), (), s32[]{:S(2)}) async-start(), calls=%async_computation.6 | async-start | bytes 8650752 | tf_op jit(solution)/shard_map/all_gather | solution.py:181
  105.5 5.7 %copy-start.7 = (f32[64,8]{0,1:T(8,128)S(1)}, f32[64,8]{0,1:T(8,128)}, u32[]{:S(2)}) copy-start(f32[64,8]{0,1:T(8,128)} %param.30) | copy-start | bytes 6148
  105.5 5.7 %copy-start.8 = (s32[64,8]{0,1:T(8,128)S(1)}, s32[64,8]{0,1:T(8,128)}, u32[]{:S(2)}) copy-start(s32[64,8]{0,1:T(8,128)} %param.29) | copy-start | bytes 6148
  105.5 5.7 %copy-start.9 = (s32[16]{0:T(128)S(1)}, s32[16]{0:T(128)}, u32[]{:S(2)}) copy-start(s32[16]{0:T(128)} %param.31) | copy-start | bytes 196
  105.5 232.6 %all-to-all-start = ((bf16[2,3,2048,256]{3,1,0,2:T(4,128)(2,1)}), bf16[2,3,2048,256]{3,1,0,2:T(4,128)(2,1)}, u32[]{:S(2)}, u32[]{:S(2)}) async-start(bf16[2,3,2048,256]{3,1,0,2:T(4,128)(2,1)} %copy.67), calls=%async_computation.2 | async-start | bytes 16777216 | tf_op jit(solution)/shard_map/all_to_all | solution.py:185
  111.2 424.7 %reduce-scatter.5.cloned.1.call-start = ((), (), s32[]{:S(2)}) async-start(), calls=%async_computation.7 | async-start | bytes 8650752 | tf_op jit(solution)/shard_map/reduce_scatter | solution.py:183
  316.9 2.8 copy-start.2
  337.2 0.7 copy-start.12
  483.5 52.4 %copy-start.3 = (f32[64,2048]{1,0:T(8,128)S(1)}, f32[64,2048]{1,0:T(8,128)}, u32[]{:S(2)}) copy-start(f32[64,2048]{1,0:T(8,128)} %reduce-scatter.3.cloned.1.call-done) | copy-start | bytes 1572868
  483.5 54.1 %copy-start.1 = (bf16[512,2048]{1,0:T(8,128)(2,1)S(1)}, bf16[512,2048]{1,0:T(8,128)(2,1)}, u32[]{:S(2)}) copy-start(bf16[512,2048]{1,0:T(8,128)(2,1)} %param.27) | copy-start | bytes 6291460
Sparse Core Ops, SparseCore 0:
  10.2 42.8 all-gather.3
  61.7 30.1 reduce-scatter.2
  95.7 203.2 all-gather.5
  337.4 198.4 reduce-scatter.4

commit v2 on v1

--- a/solution.py
+++ b/solution.py
@@ -41,14 +41,19 @@
     return (jnp.stack(chosen_blocks, axis=1), jnp.stack(chosen_requests, axis=1))
 
 
-def experts_kernel(tok_ref, gate_ref, weights_ref, out_ref):
-    rows = tok_ref[...]
-    slot_count = weights_ref.shape[0]
+def experts_kernel(first_slot_ref, tok_ref, weights_ref, out_ref):
+    slot_count, _, model_width, _ = weights_ref.shape
+    rows = tok_ref[:, :model_width]
+    codes = tok_ref[:, model_width:].astype(jnp.float32)
+    half_codes = codes.shape[1] // 2
+    lane = lax.broadcasted_iota(jnp.int32, codes.shape, 1)
     total = None
     for slot_num in range(slot_count):
+        wanted = first_slot_ref[0] + slot_num
+        picked = (lane == wanted) | (lane == wanted + half_codes)
+        factor = jnp.sum(jnp.where(picked, codes, 0.0), axis=1, keepdims=True)
         gate_act = jnp.dot(rows, weights_ref[slot_num, 0], preferred_element_type=jnp.float32)
         up_act = jnp.dot(rows, weights_ref[slot_num, 1], preferred_element_type=jnp.float32)
-        factor = gate_ref[:, slot_num : slot_num + 1]
         hidden = gate_act / (1.0 + jnp.exp(-gate_act)) * up_act
         hidden = (hidden * factor).astype(jnp.bfloat16)
         part = lax.dot_general(
@@ -61,16 +66,16 @@
     out_ref[...] = total.astype(out_ref.dtype)
 
 
-def run_experts(tokens, gates, slot_weights, block):
-    count, width = tokens.shape
-    slots_here, mats, _, hidden_size = slot_weights.shape
+def run_experts(first_slot, tokens, slot_weights, block):
+    count, ext_width = tokens.shape
+    slots_here, mats, width, hidden_size = slot_weights.shape
     return pl.pallas_call(
         experts_kernel,
         out_shape=jax.ShapeDtypeStruct((count, width), jnp.bfloat16),
         grid=(count // block,),
         in_specs=[
-            pl.BlockSpec((block, width), lambda i: (i, 0)),
-            pl.BlockSpec((block, slots_here), lambda i: (i, 0)),
+            pl.BlockSpec(memory_space=pltpu.SMEM),
+            pl.BlockSpec((block, ext_width), lambda i: (i, 0)),
             pl.BlockSpec((slots_here, mats, width, hidden_size), lambda i: (0, 0, 0, 0)),
         ],
         out_specs=pl.BlockSpec((block, width), lambda i: (i, 0)),
@@ -80,7 +85,133 @@
             bytes_accessed=4 * count * width + 2 * slot_weights.size,
             transcendentals=count * hidden_size * slots_here,
         ),
-    )(tokens, gates, slot_weights)
+    )(first_slot, tokens, slot_weights)
+
+
+def turn_pairs(value, step):
+    count = lax.axis_size("req")
+    return lax.ppermute(value, "req", [(i, (i + 2 * step) % count) for i in range(count)])
+
+
+def turn(value, step):
+    count = lax.axis_size("req")
+    return lax.ppermute(value, "req", [(i, (i + step) % count) for i in range(count)])
+
+
+def flip_pair(value):
+    count = lax.axis_size("req")
+    return lax.ppermute(value, "req", [(i, i ^ 1) for i in range(count)])
+
+
+def flip_chip(value):
+    count = lax.axis_size("exp")
+    return lax.ppermute(value, "exp", [(i, i ^ 2) for i in range(count)])
+
+
+def flip_core(value):
+    count = lax.axis_size("exp")
+    return lax.ppermute(value, "exp", [(i, i ^ 1) for i in range(count)])
+
+
+def pick(value, index, axis):
+    return lax.dynamic_index_in_dim(value, index, axis, keepdims=False)
+
+
+def add(first, second):
+    return (first.astype(jnp.float32) + second.astype(jnp.float32)).astype(jnp.bfloat16)
+
+
+def fetch_cache(cache_keys, cache_values, need_blocks):
+    me = lax.axis_index("req")
+    pair_count = lax.axis_size("req") // 2
+    cache_dev = cache_keys.shape[0]
+    mine = jnp.stack([cache_keys, cache_values], axis=1)
+    column = jnp.stack([mine] + [turn_pairs(mine, step) for step in range(1, pair_count)])
+    column = column.reshape((pair_count * cache_dev,) + mine.shape[1:])
+
+    def rows_for(wanted):
+        holder = wanted // cache_dev
+        back = (me // 2 - holder // 2) % pair_count
+        index = back * cache_dev + wanted % cache_dev
+        return jnp.stack([pick(column, index[k], 0) for k in range(cache_dev)])
+
+    mine_wanted = pick(need_blocks, me, 0)
+    from_pair = flip_pair(rows_for(pick(need_blocks, me ^ 1, 0)))
+    here = ((mine_wanted // cache_dev) ^ me) & 1
+    return jnp.where((here == 0)[:, None, None, None], rows_for(mine_wanted), from_pair)
+
+
+def sum_heads(partial_value):
+    me = lax.axis_index("exp")
+    rows, width = partial_value.shape
+    grid = partial_value.reshape(2, 2, rows // 4, width)
+    core, chip = me % 2, me // 2
+    got = flip_core(pick(grid, 1 - core, 1).astype(jnp.bfloat16))
+    level = pick(grid, core, 1) + got.astype(jnp.float32)
+    got = flip_chip(pick(level, 1 - chip, 0).astype(jnp.bfloat16))
+    return pick(level, chip, 0) + got.astype(jnp.float32)
+
+
+def spread_tokens(pieces):
+    width = pieces[0].shape[1]
+    stacked = jnp.stack(pieces)
+    cut = stacked.shape[1] // 2
+    first, second = stacked[:, :cut], stacked[:, cut:]
+    first = jnp.stack([first, flip_pair(first)])
+    second = jnp.stack([second, flip_chip(second)])
+    first_far, second_far = flip_chip(first), flip_pair(second)
+    parts = [first, first_far, second, second_far]
+    return jnp.concatenate([part.reshape(-1, width) for part in parts])
+
+
+def gather_sums(total, piece_count):
+    rows, width = total.shape
+    cut = rows // (8 * piece_count)
+    first, second = total.reshape(2, 2, 2, piece_count, cut, width)
+    first = add(first[0], flip_chip(first[1]))
+    second = add(second[0], flip_pair(second[1]))
+    first = add(first[0], flip_pair(first[1]))
+    second = add(second[0], flip_chip(second[1]))
+    return jnp.concatenate([first, second], axis=1)
+
+
+def mix(normed, codes, slot_weights):
+    pair_count = lax.axis_size("req") // 2
+    first_slot = (lax.axis_index("req") * slot_weights.shape[0]).astype(jnp.int32).reshape(1)
+    ext = jnp.concatenate([normed, codes], axis=1)
+    pieces = [ext] + [turn_pairs(ext, step) for step in range(1, pair_count)]
+    total = None
+    for begin in range(0, pair_count, 2):
+        here = spread_tokens(pieces[begin : begin + 2])
+        there = flip_core(here)
+        back = flip_core(run_experts(first_slot, there, slot_weights, 256))
+        sums = gather_sums(add(run_experts(first_slot, here, slot_weights, 256), back), 2)
+        for offset in range(2):
+            step = begin + offset
+            part = sums[offset] if step == 0 else turn_pairs(sums[offset], -step)
+            part = part.astype(jnp.float32)
+            total = part if total is None else total + part
+    return total
+
+
+def move_replicas(slot_weights, source_slot):
+    me = lax.axis_index("req")
+    count = lax.axis_size("req")
+    slots_here = slot_weights.shape[0]
+    last = slot_weights.shape[-1]
+    chunks = slot_weights.reshape(slots_here, count, -1, last)
+    held = [pick(chunks, me, 1)]
+    for step in range(1, count):
+        held.append(turn(pick(chunks, (me + step) % count, 1), step))
+    held = jnp.concatenate(held)
+    result = jnp.zeros(chunks.shape[1:], slot_weights.dtype)
+    for step in range(count):
+        slot = pick(source_slot, (me + step) % count, 0)
+        index = ((me - slot // slots_here) % count) * slots_here + slot % slots_here
+        piece = pick(held, index, 0)
+        piece = piece if step == 0 else turn(piece, step)
+        result = lax.dynamic_update_index_in_dim(result, piece, (me - step) % count, 0)
+    return result.reshape((1,) + slot_weights.shape[1:])
 
 
 def body(
@@ -127,10 +258,11 @@
     position = (offset + jnp.where(token_cached, pre_len, 0)).astype(jnp.float32)
     need_blocks, need_requests = compact(block_rows, cache_dev)
     my_requests = lax.dynamic_index_in_dim(need_requests, group_idx, 0, keepdims=False)
-    every_cache = lax.all_gather(jnp.stack([cache_keys, cache_values]), "req", axis=1, tiled=True)
-    wanted = lax.dynamic_index_in_dim(need_blocks, group_idx, 0, keepdims=False)
-    far_cache = jnp.take(every_cache, wanted, axis=1)
-    far_keys, far_values = far_cache[0], far_cache[1]
+    far_cache = fetch_cache(cache_keys, cache_values, need_blocks)
+    far_keys, far_values = far_cache[:, 0], far_cache[:, 1]
+    far_keys, far_values, slot_weights_later = lax.optimization_barrier(
+        (far_keys, far_values, slot_weights)
+    )
     query_n = prepare(query_in.reshape(tok_grp, head_count, head_size), query_gain, position)
     key_n = prepare(key_in.reshape(tok_grp, head_count, head_size), key_gain, position)
     keyset = jnp.concatenate(
@@ -154,12 +286,7 @@
     weights = (expos / jnp.sum(expos, axis=-1, keepdims=True)).astype(jnp.bfloat16)
     attended = jnp.einsum("hqk,khd->qhd", weights, valueset, preferred_element_type=jnp.float32)
     attended = attended.astype(jnp.bfloat16).reshape(tok_grp, width_q)
-    attn_out = lax.psum_scatter(
-        jnp.dot(attended, out_proj, preferred_element_type=jnp.float32),
-        "exp",
-        scatter_dimension=0,
-        tiled=True,
-    )
+    attn_out = sum_heads(jnp.dot(attended, out_proj, preferred_element_type=jnp.float32))
     residual = hidden_in.astype(jnp.float32) + attn_out
     normed = (
         residual
@@ -167,7 +294,6 @@
         * norm_gain
     ).astype(jnp.bfloat16)
     slot_total = old_slots.shape[0]
-    slots_here = slot_weights.shape[0]
     slot_range = jnp.arange(slot_total, dtype=jnp.int32)
     slot_of = jnp.sum(
         jnp.where(old_slots[None, :] == slot_range[:, None], slot_range[None, :], 0), axis=1
@@ -176,17 +302,16 @@
         jnp.where(expert_ids[:, :, None] == old_slots[None, None, :], gate_values[:, :, None], 0.0),
         axis=1,
     )
-    every_gates = lax.all_gather(dense_gates, ("req", "exp"), axis=0, tiled=True)
-    my_gates = lax.dynamic_slice_in_dim(every_gates, group_idx * slots_here, slots_here, axis=1)
-    tokens = lax.all_gather(normed, ("req", "exp"), axis=0, tiled=True)
-    mixed = run_experts(tokens, my_gates, slot_weights, tok_grp)
-    mixture = lax.psum_scatter(mixed, ("req", "exp"), scatter_dimension=0, tiled=True)
-    layer_out = (residual + mixture.astype(jnp.float32)).astype(jnp.bfloat16)
-    spread_slots = lax.all_to_all(slot_weights, "req", split_axis=2, concat_axis=0, tiled=True)
+    high_part = dense_gates.astype(jnp.bfloat16)
+    low_part = (dense_gates - high_part.astype(jnp.float32)).astype(jnp.bfloat16)
+    lanes = max(64, slot_total)
+    gap = ((0, 0), (0, lanes - slot_total))
+    codes = jnp.concatenate([jnp.pad(high_part, gap), jnp.pad(low_part, gap)], axis=1)
+    mixture = mix(normed, codes, slot_weights)
+    layer_out = (residual + mixture).astype(jnp.bfloat16)
     replica_onehot = new_replicas[:, None] == slot_range[None, :]
     source_slot = jnp.sum(jnp.where(replica_onehot, slot_of[None, :], 0), axis=1)
-    chosen_pieces = jnp.take(spread_slots, source_slot, axis=0)
-    replica_weights = lax.all_to_all(chosen_pieces, "req", split_axis=0, concat_axis=2, tiled=True)
+    replica_weights = move_replicas(slot_weights_later, source_slot)
     return (layer_out, replica_weights)
 
 

time: 545 us -> 388 us (0.71)
  blocking collectives: 335 us -> 0 us
  starting transfers between devices: 5.83 us -> 144 us
  waiting for transfers between devices: 115 us -> 135 us
  between operations: 14.1 us -> 28.8 us
  other arithmetic: 14.6 us -> 21 us
    all_gather x1 -> x0, blocking collectives: 205 us -> none  [body(): lax.all_gather(dense_gates, ('req', 'exp'), axis=0, tiled=True)]
    ppermute x0 -> x46, starting transfers between devices: none -> 144 us  [the longest x14 104 us: turn(): lax.ppermute(value, 'req', [(i, (i + step) % count) for i in range(count)])]
    ppermute x0 -> x46, waiting for transfers between devices: none -> 135 us  [the longest x14 48.2 us: turn(): lax.ppermute(value, 'req', [(i, (i + step) % count) for i in range(count)])]
    all_to_all x1 -> x0, blocking collectives: 130 us -> none  [body(): lax.all_to_all(chosen_pieces, 'req', split_axis=0, concat_axis=2, tiled=T...]
    reduce_scatter x2 -> x0, waiting for transfers between devices: 80.7 us -> none  [the longest x1 50.4 us: body(): lax.psum_scatter(mixed, ('req', 'exp'), scatter_dimension=0, tiled=True)]
    all_gather x2 -> x0, waiting for transfers between devices: 33.9 us -> none  [the longest x1 33.8 us: body(): lax.all_gather(jnp.stack([cache_keys, cache_values]), 'req', axis=1, tile...]
    all_to_all x3 -> x0, local copies, waits for them, and re-layouts: 10 us -> none  [the longest x2 8.06 us: body(): lax.all_to_all(slot_weights, 'req', split_axis=2, concat_axis=0, tiled=True)]
    gather x2 -> x0, local copies, waits for them, and re-layouts: 6.97 us -> none  [the longest x1 5.19 us: body(): chosen_pieces = jnp.take(spread_slots, source_slot, axis=0)]
  transfers between devices with their start and end apart: 5 -> 46, of which waited for: 3 -> 19; matrix products, arithmetic and copies ran while one was open for 7% -> 11% of each run, Pallas kernels for 3% -> 5%
where the time goes in v2:
time: 388 us; the launch traced here: 387 us
  starting transfers between devices  144 us (37%)
  waiting for transfers between devices  135 us (35%)
  local copies, waits for them, and re-layouts  32.7 us (8%)
  between operations  28.8 us (7%)
  other arithmetic  21 us (5%)
  Pallas kernels  20.4 us (5%)
  matrix products  5.16 us (1%)
    ppermute x14, starting transfers between devices, turn(): lax.ppermute(value, 'req', [(i, (i + step) % count) for i in range(count)])  104 us
    ppermute x14, waiting for transfers between devices, turn(): lax.ppermute(value, 'req', [(i, (i + step) % count) for i in range(count)])  48.2 us
    ppermute x9, waiting for transfers between devices, flip_pair(): return lax.ppermute(value, 'req', [(i, i ^ 1) for i in range(count)])  33.7 us
    ppermute x9, waiting for transfers between devices, turn_pairs(): lax.ppermute(value, 'req', [(i, (i + 2 * step) % count) for i in range(co...  29.9 us
    ppermute x9, waiting for transfers between devices, flip_chip(): return lax.ppermute(value, 'exp', [(i, i ^ 2) for i in range(count)])  21.6 us
    pallas_call x4, Pallas kernels, run_experts(): pl.pallas_call(experts_kernel, out_shape=jax.ShapeDtypeStruct((count, wid...  20.4 us
    ppermute x9, starting transfers between devices, flip_chip(): return lax.ppermute(value, 'exp', [(i, i ^ 2) for i in range(count)])  16 us
    unnamed x40, local copies, waits for them, and re-layouts  12.7 us
  transfers between devices with their start and end apart: 46, of which 19 were waited for; matrix products, arithmetic and copies ran while one was open for 11% of the time, Pallas kernels for 5%

profile of v2, /device:TPU:0, one launch (start us, length us, event | category | flops | bytes accessed | tf_op | source)
XLA Modules:
  0.0 386.8 jit_solution(2786736488024465386)
XLA Ops:
  0.6 1.7 fusion.69
  2.3 3.0 collective-permute-start
  5.4 2.6 collective-permute-start.1
  32.1 1.6 collective-permute-start.3
  33.8 3.3 collective-permute-done.3
  37.3 2.8 fusion.77
  40.1 1.7 fusion.6
  44.3 1.9 collective-permute-done.4
  47.6 1.6 collective-permute-start.5
  49.5 6.5 %collective-permute-done.5 = bf16[64,2048]{1,0:T(8,128)(2,1)S(1)} collective-permute-done((bf16[64,2048]{1,0:T(8,128)(2,1)S(1)}, bf16[64,2048]{1,0:T(8,128)(2,1)S(1)}, u32[]{:S(2)}, u32[]{:S(2)}) %collective-permute-start.5) | collective-permute-done | bytes 262176 | tf_op jit(solution)/shard_map/ppermute | solution.py:108
  57.5 2.8 collective-permute-start.19
  60.3 7.7 %collective-permute-done.6 = bf16[64,2176]{1,0:T(8,128)(2,1)S(1)} collective-permute-done((bf16[64,2176]{1,0:T(8,128)(2,1)S(1)}, bf16[64,2176]{1,0:T(8,128)(2,1)S(1)}, u32[]{:S(2)}, u32[]{:S(2)}) %collective-permute-start.6) | collective-permute-done | bytes 278560 | tf_op jit(solution)/shard_map/ppermute | solution.py:93
  68.0 1.6 collective-permute-start.7
  71.1 7.2 %collective-permute-done.18 = bf16[64,2176]{1,0:T(8,128)(2,1)S(1)} collective-permute-done((bf16[64,2176]{1,0:T(8,128)(2,1)S(1)}, bf16[64,2176]{1,0:T(8,128)(2,1)S(1)}, u32[]{:S(2)}, u32[]{:S(2)}) %collective-permute-start.18) | collective-permute-done | bytes 278560 | tf_op jit(solution)/shard_map/ppermute | solution.py:93
  78.3 1.6 collective-permute-start.20
  82.2 4.5 %dynamic-slice_bitcast_fusion = (bf16[2,768,256]{2,1,0:T(8,128)(2,1)S(1)}, bf16[2,768,256]{2,1,0:T(8,128)(2,1)S(1)}, bf16[2,768,256]{2,1,0:T(8,128)(2,1)}, bf16[...) fusion(bf16[2,8,768,256]{3,2,1,0:T(8,128)(2,1)} %bitcast.182, ...), kind=kLoop, calls=%fused_computation.25 | loop fusion | bytes 11010076 | tf_op jit(solution)/shard_map/jit(dynamic_index_in_dim)/squeeze | solution.py:117
  88.2 5.9 %collective-permute-start.33 = (bf16[2,768,256]{2,1,0:T(8,128)(2,1)}, bf16[2,768,256]{2,1,0:T(8,128)(2,1)}, u32[]{:S(2)}, u32[]{:S(2)}) collective-permute-start(bf16[2,768,256]{2,1,0:T(8,128)(2,1)} %get-tuple-element.38), channel_id=1, source_target_pairs={{0,8},{4,12},{8,16},{12,20},{16,24},{20,28},{24,0},{28,4},{1,9},{5... | collective-permute-start | bytes 2359304 | tf_op jit(solution)/shard_map/ppermute | solution.py:98
  96.3 18.3 %collective-permute-done.10 = bf16[2,2,32,2176]{3,2,1,0:T(8,128)(2,1)S(1)} collective-permute-done((bf16[2,2,32,2176]{3,2,1,0:T(8,128)(2,1)S(1)}, bf16[2,2,32,2176]{3,2,1,0:T(8,128)(2,1)S(1)}, u32[]{:S(2)}, u32[]{:S(2)}) %collective-permute-start.10) | collective-permute-done | bytes 557088 | tf_op jit(solution)/shard_map/ppermute | solution.py:103
  116.3 8.0 %collective-permute-start.34 = (bf16[2,768,256]{2,1,0:T(8,128)(2,1)}, bf16[2,768,256]{2,1,0:T(8,128)(2,1)}, u32[]{:S(2)}, u32[]{:S(2)}) collective-permute-start(bf16[2,768,256]{2,1,0:T(8,128)(2,1)} %get-tuple-element.37), channel_id=1, source_target_pairs={{0,12},{4,16},{8,20},{12,24},{16,28},{20,0},{24,4},{28,8},{1,13},{... | collective-permute-start | bytes 2359304 | tf_op jit(solution)/shard_map/ppermute | solution.py:98
  146.7 47.8 %collective-permute-start.36 = (bf16[2,768,256]{2,1,0:T(8,128)(2,1)}, bf16[2,768,256]{2,1,0:T(8,128)(2,1)S(1)}, u32[]{:S(2)}, u32[]{:S(2)}) collective-permute-start(bf16[2,768,256]{2,1,0:T(8,128)(2,1)} %get-tuple-element.35), channel_id=1, source_target_pairs={{0,20},{4,24},{8,28},{12,0},{16,4},{20,8},{24,12},{28,16},{1,21},{... | collective-permute-start | bytes 2359304 | tf_op jit(solution)/shard_map/ppermute | solution.py:98
  194.5 2.8 pad_maximum_fusion.1.tok_ref
  203.6 6.1 %collective-permute-done.36 = bf16[2,768,256]{2,1,0:T(8,128)(2,1)S(1)} collective-permute-done((bf16[2,768,256]{2,1,0:T(8,128)(2,1)}, bf16[2,768,256]{2,1,0:T(8,128)(2,1)S(1)}, u32[]{:S(2)}, u32[]{:S(2)}) %collective-permute-start.36) | collective-permute-done | bytes 786464 | tf_op jit(solution)/shard_map/ppermute | solution.py:98
  209.8 9.0 %collective-permute-done.37 = bf16[2,768,256]{2,1,0:T(8,128)(2,1)S(1)} collective-permute-done((bf16[2,768,256]{2,1,0:T(8,128)(2,1)S(1)}, bf16[2,768,256]{2,1,0:T(8,128)(2,1)S(1)}, u32[]{:S(2)}, u32[]{:S(2)}) %collective-permute-start.37) | collective-permute-done | bytes 786464 | tf_op jit(solution)/shard_map/ppermute | solution.py:98
  218.8 8.4 %collective-permute-done.38 = bf16[2,768,256]{2,1,0:T(8,128)(2,1)S(1)} collective-permute-done((bf16[2,768,256]{2,1,0:T(8,128)(2,1)S(1)}, bf16[2,768,256]{2,1,0:T(8,128)(2,1)S(1)}, u32[]{:S(2)}, u32[]{:S(2)}) %collective-permute-start.38) | collective-permute-done | bytes 786464 | tf_op jit(solution)/shard_map/ppermute | solution.py:98
  227.3 1.9 broadcast_in_dim.181
  230.6 15.9 %collective-permute-start.40 = (bf16[768,256]{1,0:T(8,128)(2,1)}, bf16[768,256]{1,0:T(8,128)(2,1)S(1)}, u32[]{:S(2)}, u32[]{:S(2)}) collective-permute-start(bf16[768,256]{1,0:T(8,128)(2,1)} %get-tuple-element.30), channel_id=1, source_target_pairs={{0,8},{4,12},{8,16},{12,20},{16,24},{20,28},{24,0},{28,4},{1,9},{5... | collective-permute-start | bytes 1179656 | tf_op jit(solution)/shard_map/ppermute | solution.py:98
  246.4 4.8 %collective-permute-start.42 = (bf16[768,256]{1,0:T(8,128)(2,1)}, bf16[768,256]{1,0:T(8,128)(2,1)S(1)}, u32[]{:S(2)}, u32[]{:S(2)}) collective-permute-start(bf16[768,256]{1,0:T(8,128)(2,1)} %get-tuple-element.28), channel_id=1, source_target_pairs={{0,16},{4,20},{8,24},{12,28},{16,0},{20,4},{24,8},{28,12},{1,17},{... | collective-permute-start | bytes 1179656 | tf_op jit(solution)/shard_map/ppermute | solution.py:98
  251.2 2.8 copy-done.2
  254.0 5.1 %shard_map.177 = bf16[512,2048]{1,0:T(8,128)(2,1)S(1)} custom-call(s32[1]{0:T(128)} %bitcast.34.first_slot_ref, bf16[512,2176]{1,0:T(8,128)(2,1)} %collective-permute-done.11.tok_ref, bf16[2,3,2048,256]{3,2,1,0:T(8,128)(2,1)S(1)} %copy-done.2), custom_call_target="tpu_custom_call" | custom-call | flops 3221225472 | bytes 10485760 | tf_op jit(solution)/shard_map/pallas_call | solution.py:72
  260.0 1.8 bitcast_dynamic-update-slice_fusion.7
  261.7 5.9 %collective-permute-start.43 = (bf16[768,256]{1,0:T(8,128)(2,1)S(1)}, bf16[768,256]{1,0:T(8,128)(2,1)S(1)}, u32[]{:S(2)}, u32[]{:S(2)}) collective-permute-start(bf16[768,256]{1,0:T(8,128)(2,1)S(1)} %copy-done.4), channel_id=1, source_target_pairs={{0,20},{4,24},{8,28},{12,0},{16,4},{20,8},{24,12},{28,16},{1,21},{... | collective-permute-start | bytes 1179656 | tf_op jit(solution)/shard_map/ppermute | solution.py:98
  268.4 23.8 %collective-permute-done.41 = bf16[768,256]{1,0:T(8,128)(2,1)S(1)} collective-permute-done((bf16[768,256]{1,0:T(8,128)(2,1)}, bf16[768,256]{1,0:T(8,128)(2,1)S(1)}, u32[]{:S(2)}, u32[]{:S(2)}) %collective-permute-start.41) | collective-permute-done | bytes 393248 | tf_op jit(solution)/shard_map/ppermute | solution.py:98
  292.2 12.5 %collective-permute-start.44 = (bf16[768,256]{1,0:T(8,128)(2,1)S(1)}, bf16[768,256]{1,0:T(8,128)(2,1)S(1)}, u32[]{:S(2)}, u32[]{:S(2)}) collective-permute-start(bf16[768,256]{1,0:T(8,128)(2,1)S(1)} %get-tuple-element.26), channel_id=1, source_target_pairs={{0,24},{4,28},{8,0},{12,4},{16,8},{20,12},{24,16},{28,20},{1,25},{... | collective-permute-start | bytes 1179656 | tf_op jit(solution)/shard_map/ppermute | solution.py:98
  305.6 5.1 %shard_map.179 = bf16[512,2048]{1,0:T(8,128)(2,1)S(1)} custom-call(s32[1]{0:T(128)} %bitcast.34.first_slot_ref, bf16[512,2176]{1,0:T(8,128)(2,1)} %collective-permute-done.24.tok_ref, bf16[2,3,2048,256]{3,2,1,0:T(8,128)(2,1)S(1)} %copy-done.2), custom_call_target="tpu_custom_call" | custom-call | flops 3221225472 | bytes 10485760 | tf_op jit(solution)/shard_map/pallas_call | solution.py:72
  312.3 5.1 %shard_map.176 = bf16[512,2048]{1,0:T(8,128)(2,1)S(1)} custom-call(s32[1]{0:T(128)} %bitcast.34.first_slot_ref, bf16[512,2176]{1,0:T(8,128)(2,1)} %pad_maximum_fusion.tok_ref, bf16[2,3,2048,256]{3,2,1,0:T(8,128)(2,1)S(1)} %copy-done.2), custom_call_target="tpu_custom_call" | custom-call | flops 3221225472 | bytes 10485760 | tf_op jit(solution)/shard_map/pallas_call | solution.py:72
  317.4 5.1 %shard_map.178 = bf16[512,2048]{1,0:T(8,128)(2,1)S(1)} custom-call(s32[1]{0:T(128)} %bitcast.34.first_slot_ref, bf16[512,2176]{1,0:T(8,128)(2,1)} %pad_maximum_fusion.1.tok_ref, bf16[2,3,2048,256]{3,2,1,0:T(8,128)(2,1)S(1)} %copy-done.2), custom_call_target="tpu_custom_call" | custom-call | flops 3221225472 | bytes 10485760 | tf_op jit(solution)/shard_map/pallas_call | solution.py:72
  323.5 5.5 %collective-permute-start.13 = (bf16[2,2,32,2048]{3,2,1,0:T(8,128)(2,1)S(1)}, bf16[2,2,32,2048]{3,2,1,0:T(8,128)(2,1)S(1)}, u32[]{:S(2)}, u32[]{:S(2)}) collective-permute-start(bf16[2,2,32,2048]{3,2,1,0:T(8,128)(2,1)S(1)} %bitcast.206), channel_id=1, source_target_pairs={{0,2},{1,3},{2,0},{3,1},{4,6},{5,7},{6,4},{7,5},{8,10},{9,11},{10,... | collective-permute-start | bytes 1572872 | tf_op jit(solution)/shard_map/ppermute | solution.py:108
  329.0 2.0 collective-permute-start.15
  332.1 9.5 %collective-permute-done.13 = bf16[2,2,32,2048]{3,2,1,0:T(8,128)(2,1)S(1)} collective-permute-done((bf16[2,2,32,2048]{3,2,1,0:T(8,128)(2,1)S(1)}, bf16[2,2,32,2048]{3,2,1,0:T(8,128)(2,1)S(1)}, u32[]{:S(2)}, u32[]{:S(2)}) %collective-permute-start.13) | collective-permute-done | bytes 524320 | tf_op jit(solution)/shard_map/ppermute | solution.py:108
  341.5 1.7 collective-permute-start.26
  343.7 2.1 collective-permute-start.14
  345.9 9.0 %collective-permute-done.28 = bf16[2,2,32,2048]{3,2,1,0:T(8,128)(2,1)S(1)} collective-permute-done((bf16[2,2,32,2048]{3,2,1,0:T(8,128)(2,1)S(1)}, bf16[2,2,32,2048]{3,2,1,0:T(8,128)(2,1)S(1)}, u32[]{:S(2)}, u32[]{:S(2)}) %collective-permute-start.28) | collective-permute-done | bytes 524320 | tf_op jit(solution)/shard_map/ppermute | solution.py:103
  355.3 1.9 collective-permute-start.29
  357.3 2.8 collective-permute-done.14
  360.1 1.7 collective-permute-start.27
  361.9 2.2 collective-permute-done.16
  364.7 3.3 collective-permute-done.29
  370.9 15.1 %collective-permute-done.30 = bf16[64,2048]{1,0:T(8,128)(2,1)S(1)} collective-permute-done((bf16[64,2048]{1,0:T(8,128)(2,1)S(1)}, bf16[64,2048]{1,0:T(8,128)(2,1)S(1)}, u32[]{:S(2)}, u32[]{:S(2)}) %collective-permute-start.30) | collective-permute-done | bytes 262176 | tf_op jit(solution)/shard_map/ppermute | solution.py:93
  (188 shorter events, 53.2 us)
Async XLA Ops:
  0.6 41.4 %copy-start = (bf16[512,2048]{1,0:T(8,128)(2,1)S(1)}, bf16[512,2048]{1,0:T(8,128)(2,1)}, u32[]{:S(2)}) copy-start(bf16[512,2048]{1,0:T(8,128)(2,1)} %param.27) | copy-start | bytes 6291460
  2.3 28.5 %collective-permute-start = (bf16[2,2,32,512]{3,2,1,0:T(8,128)(2,1)}, bf16[2,2,32,512]{3,2,1,0:T(8,128)(2,1)}, u32[]{:S(2)}, u32[]{:S(2)}) collective-permute-start(bf16[2,2,32,512]{3,2,1,0:T(8,128)(2,1)} %get-tuple-element.67), channel_id=1, source_target_pairs={{0,8},{4,12},{8,16},{12,20},{16,24},{20,28},{24,0},{28,4},{1,9},{5... | collective-permute-start | bytes 393224 | tf_op jit(solution)/shard_map/ppermute | solution.py:93
  5.4 25.5 %collective-permute-start.1 = (bf16[2,2,32,512]{3,2,1,0:T(8,128)(2,1)}, bf16[2,2,32,512]{3,2,1,0:T(8,128)(2,1)}, u32[]{:S(2)}, u32[]{:S(2)}) collective-permute-start(bf16[2,2,32,512]{3,2,1,0:T(8,128)(2,1)} %get-tuple-element.67), channel_id=1, source_target_pairs={{0,16},{4,20},{8,24},{12,28},{16,0},{20,4},{24,8},{28,12},{1,17},{... | collective-permute-start | bytes 393224 | tf_op jit(solution)/shard_map/ppermute | solution.py:93
  8.0 22.9 %collective-permute-start.2 = (bf16[2,2,32,512]{3,2,1,0:T(8,128)(2,1)}, bf16[2,2,32,512]{3,2,1,0:T(8,128)(2,1)}, u32[]{:S(2)}, u32[]{:S(2)}) collective-permute-start(bf16[2,2,32,512]{3,2,1,0:T(8,128)(2,1)} %get-tuple-element.67), channel_id=1, source_target_pairs={{0,24},{4,28},{8,0},{12,4},{16,8},{20,12},{24,16},{28,20},{1,25},{... | collective-permute-start | bytes 393224 | tf_op jit(solution)/shard_map/ppermute | solution.py:93
  32.1 5.0 %collective-permute-start.3 = (bf16[2,2,32,512]{3,2,1,0:T(8,128)(2,1)S(1)}, bf16[2,2,32,512]{3,2,1,0:T(8,128)(2,1)S(1)}, u32[]{:S(2)}, u32[]{:S(2)}) collective-permute-start(bf16[2,2,32,512]{3,2,1,0:T(8,128)(2,1)S(1)} %pad_maximum_fusion.12), channel_id=1, source_target_pairs={{0,4},{4,0},{8,12},{12,8},{16,20},{20,16},{24,28},{28,24},{1,5},{5... | collective-permute-start | bytes 393224 | tf_op jit(solution)/shard_map/ppermute | solution.py:103
  44.2 2.0 collective-permute-start.4
  47.6 8.4 %collective-permute-start.5 = (bf16[64,2048]{1,0:T(8,128)(2,1)S(1)}, bf16[64,2048]{1,0:T(8,128)(2,1)S(1)}, u32[]{:S(2)}, u32[]{:S(2)}) collective-permute-start(bf16[64,2048]{1,0:T(8,128)(2,1)S(1)} %fusion.31), channel_id=1, source_target_pairs={{0,2},{1,3},{2,0},{3,1},{4,6},{5,7},{6,4},{7,5},{8,10},{9,11},{10,... | collective-permute-start | bytes 786440 | tf_op jit(solution)/shard_map/ppermute | solution.py:108
  56.4 11.5 %collective-permute-start.6 = (bf16[64,2176]{1,0:T(8,128)(2,1)S(1)}, bf16[64,2176]{1,0:T(8,128)(2,1)S(1)}, u32[]{:S(2)}, u32[]{:S(2)}) collective-permute-start(bf16[64,2176]{1,0:T(8,128)(2,1)S(1)} %concatenate.40), channel_id=1, source_target_pairs={{0,8},{4,12},{8,16},{12,20},{16,24},{20,28},{24,0},{28,4},{1,9},{5... | collective-permute-start | bytes 835592 | tf_op jit(solution)/shard_map/ppermute | solution.py:93
  57.2 21.1 %collective-permute-start.18 = (bf16[64,2176]{1,0:T(8,128)(2,1)S(1)}, bf16[64,2176]{1,0:T(8,128)(2,1)S(1)}, u32[]{:S(2)}, u32[]{:S(2)}) collective-permute-start(bf16[64,2176]{1,0:T(8,128)(2,1)S(1)} %concatenate.40), channel_id=1, source_target_pairs={{0,16},{4,20},{8,24},{12,28},{16,0},{20,4},{24,8},{28,12},{1,17},{... | collective-permute-start | bytes 835592 | tf_op jit(solution)/shard_map/ppermute | solution.py:93
  57.5 20.8 %collective-permute-start.19 = (bf16[64,2176]{1,0:T(8,128)(2,1)S(1)}, bf16[64,2176]{1,0:T(8,128)(2,1)S(1)}, u32[]{:S(2)}, u32[]{:S(2)}) collective-permute-start(bf16[64,2176]{1,0:T(8,128)(2,1)S(1)} %concatenate.40), channel_id=1, source_target_pairs={{0,24},{4,28},{8,0},{12,4},{16,8},{20,12},{24,16},{28,20},{1,25},{... | collective-permute-start | bytes 835592 | tf_op jit(solution)/shard_map/ppermute | solution.py:93
  68.0 11.9 %collective-permute-start.7 = (bf16[2,32,2176]{2,1,0:T(8,128)(2,1)S(1)}, bf16[2,32,2176]{2,1,0:T(8,128)(2,1)S(1)}, u32[]{:S(2)}, u32[]{:S(2)}) collective-permute-start(bf16[2,32,2176]{2,1,0:T(8,128)(2,1)S(1)} %get-tuple-element.52), channel_id=1, source_target_pairs={{0,4},{4,0},{8,12},{12,8},{16,20},{20,16},{24,28},{28,24},{1,5},{5... | collective-permute-start | bytes 835592 | tf_op jit(solution)/shard_map/ppermute | solution.py:103
  69.6 12.0 %collective-permute-start.9 = (bf16[2,32,2176]{2,1,0:T(8,128)(2,1)S(1)}, bf16[2,32,2176]{2,1,0:T(8,128)(2,1)S(1)}, u32[]{:S(2)}, u32[]{:S(2)}) collective-permute-start(bf16[2,32,2176]{2,1,0:T(8,128)(2,1)S(1)} %get-tuple-element.53), channel_id=1, source_target_pairs={{0,2},{1,3},{2,0},{3,1},{4,6},{5,7},{6,4},{7,5},{8,10},{9,11},{10,... | collective-permute-start | bytes 835592 | tf_op jit(solution)/shard_map/ppermute | solution.py:108
  78.3 15.8 %collective-permute-start.20 = (bf16[2,32,2176]{2,1,0:T(8,128)(2,1)S(1)}, bf16[2,32,2176]{2,1,0:T(8,128)(2,1)S(1)}, u32[]{:S(2)}, u32[]{:S(2)}) collective-permute-start(bf16[2,32,2176]{2,1,0:T(8,128)(2,1)S(1)} %get-tuple-element.54), channel_id=1, source_target_pairs={{0,4},{4,0},{8,12},{12,8},{16,20},{20,16},{24,28},{28,24},{1,5},{5... | collective-permute-start | bytes 835592 | tf_op jit(solution)/shard_map/ppermute | solution.py:103
  80.0 14.7 %collective-permute-start.8 = (bf16[2,2,32,2176]{3,2,1,0:T(8,128)(2,1)S(1)}, bf16[2,2,32,2176]{3,2,1,0:T(8,128)(2,1)S(1)}, u32[]{:S(2)}, u32[]{:S(2)}) collective-permute-start(bf16[2,2,32,2176]{3,2,1,0:T(8,128)(2,1)S(1)} %pad_maximum_fusion.2), channel_id=1, source_target_pairs={{0,2},{1,3},{2,0},{3,1},{4,6},{5,7},{6,4},{7,5},{8,10},{9,11},{10,... | collective-permute-start | bytes 1671176 | tf_op jit(solution)/shard_map/ppermute | solution.py:108
  81.6 32.9 %collective-permute-start.10 = (bf16[2,2,32,2176]{3,2,1,0:T(8,128)(2,1)S(1)}, bf16[2,2,32,2176]{3,2,1,0:T(8,128)(2,1)S(1)}, u32[]{:S(2)}, u32[]{:S(2)}) collective-permute-start(bf16[2,2,32,2176]{3,2,1,0:T(8,128)(2,1)S(1)} %pad_maximum_fusion.3), channel_id=1, source_target_pairs={{0,4},{4,0},{8,12},{12,8},{16,20},{20,16},{24,28},{28,24},{1,5},{5... | collective-permute-start | bytes 1671176 | tf_op jit(solution)/shard_map/ppermute | solution.py:103
  86.7 29.5 %collective-permute-start.32 = (bf16[2,768,256]{2,1,0:T(8,128)(2,1)}, bf16[2,768,256]{2,1,0:T(8,128)(2,1)}, u32[]{:S(2)}, u32[]{:S(2)}) collective-permute-start(bf16[2,768,256]{2,1,0:T(8,128)(2,1)} %get-tuple-element.39), channel_id=1, source_target_pairs={{0,4},{4,8},{8,12},{12,16},{16,20},{20,24},{24,28},{28,0},{1,5},{5... | collective-permute-start | bytes 2359304 | tf_op jit(solution)/shard_map/ppermute | solution.py:98
  88.2 36.0 %collective-permute-start.33 = (bf16[2,768,256]{2,1,0:T(8,128)(2,1)}, bf16[2,768,256]{2,1,0:T(8,128)(2,1)}, u32[]{:S(2)}, u32[]{:S(2)}) collective-permute-start(bf16[2,768,256]{2,1,0:T(8,128)(2,1)} %get-tuple-element.38), channel_id=1, source_target_pairs={{0,8},{4,12},{8,16},{12,20},{16,24},{20,28},{24,0},{28,4},{1,9},{5... | collective-permute-start | bytes 2359304 | tf_op jit(solution)/shard_map/ppermute | solution.py:98
  94.1 22.0 %collective-permute-start.22 = (bf16[2,32,2176]{2,1,0:T(8,128)(2,1)S(1)}, bf16[2,32,2176]{2,1,0:T(8,128)(2,1)S(1)}, u32[]{:S(2)}, u32[]{:S(2)}) collective-permute-start(bf16[2,32,2176]{2,1,0:T(8,128)(2,1)S(1)} %get-tuple-element.55), channel_id=1, source_target_pairs={{0,2},{1,3},{2,0},{3,1},{4,6},{5,7},{6,4},{7,5},{8,10},{9,11},{10,... | collective-permute-start | bytes 835592 | tf_op jit(solution)/shard_map/ppermute | solution.py:108
  94.7 29.7 %copy-start.13 = (s32[8]{0:T(128)S(1)}, s32[8]{0:T(128)}, u32[]{:S(2)}) copy-start(s32[8]{0:T(128)} %param.32) | copy-start | bytes 100
  94.7 51.9 %collective-permute-start.21 = (bf16[2,2,32,2176]{3,2,1,0:T(8,128)(2,1)S(1)}, bf16[2,2,32,2176]{3,2,1,0:T(8,128)(2,1)}, u32[]{:S(2)}, u32[]{:S(2)}) collective-permute-start(bf16[2,2,32,2176]{3,2,1,0:T(8,128)(2,1)S(1)} %pad_maximum_fusion.4), channel_id=1, source_target_pairs={{0,2},{1,3},{2,0},{3,1},{4,6},{5,7},{6,4},{7,5},{8,10},{9,11},{10,... | collective-permute-start | bytes 1671176 | tf_op jit(solution)/shard_map/ppermute | solution.py:108
  116.1 130.3 %collective-permute-start.11 = (bf16[512,2176]{1,0:T(8,128)(2,1)}, bf16[512,2176]{1,0:T(8,128)(2,1)}, u32[]{:S(2)}, u32[]{:S(2)}) collective-permute-start(bf16[512,2176]{1,0:T(8,128)(2,1)} %pad_maximum_fusion.tok_ref), channel_id=1, source_target_pairs={{0,1},{1,0},{2,3},{3,2},{4,5},{5,4},{6,7},{7,6},{8,9},{9,8},{10,11... | collective-permute-start | bytes 6684680 | tf_op jit(solution)/shard_map/ppermute | solution.py:113
  116.2 78.3 %collective-permute-start.23 = (bf16[2,2,32,2176]{3,2,1,0:T(8,128)(2,1)S(1)}, bf16[2,2,32,2176]{3,2,1,0:T(8,128)(2,1)}, u32[]{:S(2)}, u32[]{:S(2)}) collective-permute-start(bf16[2,2,32,2176]{3,2,1,0:T(8,128)(2,1)S(1)} %pad_maximum_fusion.5), channel_id=1, source_target_pairs={{0,4},{4,0},{8,12},{12,8},{16,20},{20,16},{24,28},{28,24},{1,5},{5... | collective-permute-start | bytes 1671176 | tf_op jit(solution)/shard_map/ppermute | solution.py:103
  116.3 81.0 %collective-permute-start.34 = (bf16[2,768,256]{2,1,0:T(8,128)(2,1)}, bf16[2,768,256]{2,1,0:T(8,128)(2,1)}, u32[]{:S(2)}, u32[]{:S(2)}) collective-permute-start(bf16[2,768,256]{2,1,0:T(8,128)(2,1)} %get-tuple-element.37), channel_id=1, source_target_pairs={{0,12},{4,16},{8,20},{12,24},{16,28},{20,0},{24,4},{28,8},{1,13},{... | collective-permute-start | bytes 2359304 | tf_op jit(solution)/shard_map/ppermute | solution.py:98
  124.2 74.6 %collective-permute-start.35 = (bf16[2,768,256]{2,1,0:T(8,128)(2,1)}, bf16[2,768,256]{2,1,0:T(8,128)(2,1)}, u32[]{:S(2)}, u32[]{:S(2)}) collective-permute-start(bf16[2,768,256]{2,1,0:T(8,128)(2,1)} %get-tuple-element.36), channel_id=1, source_target_pairs={{0,16},{4,20},{8,24},{12,28},{16,0},{20,4},{24,8},{28,12},{1,17},{... | collective-permute-start | bytes 2359304 | tf_op jit(solution)/shard_map/ppermute | solution.py:98
  146.7 63.0 %collective-permute-start.36 = (bf16[2,768,256]{2,1,0:T(8,128)(2,1)}, bf16[2,768,256]{2,1,0:T(8,128)(2,1)S(1)}, u32[]{:S(2)}, u32[]{:S(2)}) collective-permute-start(bf16[2,768,256]{2,1,0:T(8,128)(2,1)} %get-tuple-element.35), channel_id=1, source_target_pairs={{0,20},{4,24},{8,28},{12,0},{16,4},{20,8},{24,12},{28,16},{1,21},{... | collective-permute-start | bytes 2359304 | tf_op jit(solution)/shard_map/ppermute | solution.py:98
  194.5 24.3 %collective-permute-start.37 = (bf16[2,768,256]{2,1,0:T(8,128)(2,1)S(1)}, bf16[2,768,256]{2,1,0:T(8,128)(2,1)S(1)}, u32[]{:S(2)}, u32[]{:S(2)}) collective-permute-start(bf16[2,768,256]{2,1,0:T(8,128)(2,1)S(1)} %get-tuple-element.34), channel_id=1, source_target_pairs={{0,24},{4,28},{8,0},{12,4},{16,8},{20,12},{24,16},{28,20},{1,25},{... | collective-permute-start | bytes 2359304 | tf_op jit(solution)/shard_map/ppermute | solution.py:98
  197.3 29.9 %collective-permute-start.38 = (bf16[2,768,256]{2,1,0:T(8,128)(2,1)S(1)}, bf16[2,768,256]{2,1,0:T(8,128)(2,1)S(1)}, u32[]{:S(2)}, u32[]{:S(2)}) collective-permute-start(bf16[2,768,256]{2,1,0:T(8,128)(2,1)S(1)} %get-tuple-element.33), channel_id=1, source_target_pairs={{0,28},{4,0},{8,4},{12,8},{16,12},{20,16},{24,20},{28,24},{1,29},{... | collective-permute-start | bytes 2359304 | tf_op jit(solution)/shard_map/ppermute | solution.py:98
  198.8 106.7 %collective-permute-start.24 = (bf16[512,2176]{1,0:T(8,128)(2,1)}, bf16[512,2176]{1,0:T(8,128)(2,1)}, u32[]{:S(2)}, u32[]{:S(2)}) collective-permute-start(bf16[512,2176]{1,0:T(8,128)(2,1)} %pad_maximum_fusion.1.tok_ref), channel_id=1, source_target_pairs={{0,1},{1,0},{2,3},{3,2},{4,5},{5,4},{6,7},{7,6},{8,9},{9,8},{10,11... | collective-permute-start | bytes 6684680 | tf_op jit(solution)/shard_map/ppermute | solution.py:113
  230.6 29.4 %collective-permute-start.39 = (bf16[768,256]{1,0:T(8,128)(2,1)}, bf16[768,256]{1,0:T(8,128)(2,1)}, u32[]{:S(2)}, u32[]{:S(2)}) collective-permute-start(bf16[768,256]{1,0:T(8,128)(2,1)} %get-tuple-element.31), channel_id=1, source_target_pairs={{0,4},{4,8},{8,12},{12,16},{16,20},{20,24},{24,28},{28,0},{1,5},{5... | collective-permute-start | bytes 1179656 | tf_op jit(solution)/shard_map/ppermute | solution.py:98
  230.6 31.2 %collective-permute-start.40 = (bf16[768,256]{1,0:T(8,128)(2,1)}, bf16[768,256]{1,0:T(8,128)(2,1)S(1)}, u32[]{:S(2)}, u32[]{:S(2)}) collective-permute-start(bf16[768,256]{1,0:T(8,128)(2,1)} %get-tuple-element.30), channel_id=1, source_target_pairs={{0,8},{4,12},{8,16},{12,20},{16,24},{20,28},{24,0},{28,4},{1,9},{5... | collective-permute-start | bytes 1179656 | tf_op jit(solution)/shard_map/ppermute | solution.py:98
  246.4 45.8 %collective-permute-start.41 = (bf16[768,256]{1,0:T(8,128)(2,1)}, bf16[768,256]{1,0:T(8,128)(2,1)S(1)}, u32[]{:S(2)}, u32[]{:S(2)}) collective-permute-start(bf16[768,256]{1,0:T(8,128)(2,1)} %get-tuple-element.29), channel_id=1, source_target_pairs={{0,12},{4,16},{8,20},{12,24},{16,28},{20,0},{24,4},{28,8},{1,13},{... | collective-permute-start | bytes 1179656 | tf_op jit(solution)/shard_map/ppermute | solution.py:98
  246.4 64.2 %collective-permute-start.42 = (bf16[768,256]{1,0:T(8,128)(2,1)}, bf16[768,256]{1,0:T(8,128)(2,1)S(1)}, u32[]{:S(2)}, u32[]{:S(2)}) collective-permute-start(bf16[768,256]{1,0:T(8,128)(2,1)} %get-tuple-element.28), channel_id=1, source_target_pairs={{0,16},{4,20},{8,24},{12,28},{16,0},{20,4},{24,8},{28,12},{1,17},{... | collective-permute-start | bytes 1179656 | tf_op jit(solution)/shard_map/ppermute | solution.py:98
  260.0 62.5 %collective-permute-start.12 = (bf16[512,2048]{1,0:T(8,128)(2,1)S(1)}, bf16[512,2048]{1,0:T(8,128)(2,1)S(1)}, u32[]{:S(2)}, u32[]{:S(2)}) collective-permute-start(bf16[512,2048]{1,0:T(8,128)(2,1)S(1)} %shard_map.177), channel_id=1, source_target_pairs={{0,1},{1,0},{2,3},{3,2},{4,5},{5,4},{6,7},{7,6},{8,9},{9,8},{10,11... | collective-permute-start | bytes 6291464 | tf_op jit(solution)/shard_map/ppermute | solution.py:113
  261.7 49.8 %collective-permute-start.43 = (bf16[768,256]{1,0:T(8,128)(2,1)S(1)}, bf16[768,256]{1,0:T(8,128)(2,1)S(1)}, u32[]{:S(2)}, u32[]{:S(2)}) collective-permute-start(bf16[768,256]{1,0:T(8,128)(2,1)S(1)} %copy-done.4), channel_id=1, source_target_pairs={{0,20},{4,24},{8,28},{12,0},{16,4},{20,8},{24,12},{28,16},{1,21},{... | collective-permute-start | bytes 1179656 | tf_op jit(solution)/shard_map/ppermute | solution.py:98
  292.2 77.1 %collective-permute-start.44 = (bf16[768,256]{1,0:T(8,128)(2,1)S(1)}, bf16[768,256]{1,0:T(8,128)(2,1)S(1)}, u32[]{:S(2)}, u32[]{:S(2)}) collective-permute-start(bf16[768,256]{1,0:T(8,128)(2,1)S(1)} %get-tuple-element.26), channel_id=1, source_target_pairs={{0,24},{4,28},{8,0},{12,4},{16,8},{20,12},{24,16},{28,20},{1,25},{... | collective-permute-start | bytes 1179656 | tf_op jit(solution)/shard_map/ppermute | solution.py:98
  305.6 64.5 %collective-permute-start.45 = (bf16[768,256]{1,0:T(8,128)(2,1)S(1)}, bf16[768,256]{1,0:T(8,128)(2,1)S(1)}, u32[]{:S(2)}, u32[]{:S(2)}) collective-permute-start(bf16[768,256]{1,0:T(8,128)(2,1)S(1)} %get-tuple-element.25), channel_id=1, source_target_pairs={{0,28},{4,0},{8,4},{12,8},{16,12},{20,16},{24,20},{28,24},{1,29},{... | collective-permute-start | bytes 1179656 | tf_op jit(solution)/shard_map/ppermute | solution.py:98
  310.7 20.3 %collective-permute-start.25 = (bf16[512,2048]{1,0:T(8,128)(2,1)S(1)}, bf16[512,2048]{1,0:T(8,128)(2,1)S(1)}, u32[]{:S(2)}, u32[]{:S(2)}) collective-permute-start(bf16[512,2048]{1,0:T(8,128)(2,1)S(1)} %shard_map.179), channel_id=1, source_target_pairs={{0,1},{1,0},{2,3},{3,2},{4,5},{5,4},{6,7},{7,6},{8,9},{9,8},{10,11... | collective-permute-start | bytes 6291464 | tf_op jit(solution)/shard_map/ppermute | solution.py:113
  323.5 18.1 %collective-permute-start.13 = (bf16[2,2,32,2048]{3,2,1,0:T(8,128)(2,1)S(1)}, bf16[2,2,32,2048]{3,2,1,0:T(8,128)(2,1)S(1)}, u32[]{:S(2)}, u32[]{:S(2)}) collective-permute-start(bf16[2,2,32,2048]{3,2,1,0:T(8,128)(2,1)S(1)} %bitcast.206), channel_id=1, source_target_pairs={{0,2},{1,3},{2,0},{3,1},{4,6},{5,7},{6,4},{7,5},{8,10},{9,11},{10,... | collective-permute-start | bytes 1572872 | tf_op jit(solution)/shard_map/ppermute | solution.py:108
  329.0 14.7 %collective-permute-start.15 = (bf16[2,2,32,2048]{3,2,1,0:T(8,128)(2,1)S(1)}, bf16[2,2,32,2048]{3,2,1,0:T(8,128)(2,1)S(1)}, u32[]{:S(2)}, u32[]{:S(2)}) collective-permute-start(bf16[2,2,32,2048]{3,2,1,0:T(8,128)(2,1)S(1)} %bitcast.204), channel_id=1, source_target_pairs={{0,4},{4,0},{8,12},{12,8},{16,20},{20,16},{24,28},{28,24},{1,5},{5... | collective-permute-start | bytes 1572872 | tf_op jit(solution)/shard_map/ppermute | solution.py:103
  332.0 22.9 %collective-permute-start.28 = (bf16[2,2,32,2048]{3,2,1,0:T(8,128)(2,1)S(1)}, bf16[2,2,32,2048]{3,2,1,0:T(8,128)(2,1)S(1)}, u32[]{:S(2)}, u32[]{:S(2)}) collective-permute-start(bf16[2,2,32,2048]{3,2,1,0:T(8,128)(2,1)S(1)} %bitcast.205), channel_id=1, source_target_pairs={{0,4},{4,0},{8,12},{12,8},{16,20},{20,16},{24,28},{28,24},{1,5},{5... | collective-permute-start | bytes 1572872 | tf_op jit(solution)/shard_map/ppermute | solution.py:103
  341.5 13.7 %collective-permute-start.26 = (bf16[2,2,32,2048]{3,2,1,0:T(8,128)(2,1)S(1)}, bf16[2,2,32,2048]{3,2,1,0:T(8,128)(2,1)S(1)}, u32[]{:S(2)}, u32[]{:S(2)}) collective-permute-start(bf16[2,2,32,2048]{3,2,1,0:T(8,128)(2,1)S(1)} %bitcast.203), channel_id=1, source_target_pairs={{0,2},{1,3},{2,0},{3,1},{4,6},{5,7},{6,4},{7,5},{8,10},{9,11},{10,... | collective-permute-start | bytes 1572872 | tf_op jit(solution)/shard_map/ppermute | solution.py:108
  343.7 16.5 %collective-permute-start.14 = (bf16[2,32,2048]{2,1,0:T(8,128)(2,1)S(1)}, bf16[2,32,2048]{2,1,0:T(8,128)(2,1)S(1)}, u32[]{:S(2)}, u32[]{:S(2)}) collective-permute-start(bf16[2,32,2048]{2,1,0:T(8,128)(2,1)S(1)} %slice_bitcast_fusion.6), channel_id=1, source_target_pairs={{0,4},{4,0},{8,12},{12,8},{16,20},{20,16},{24,28},{28,24},{1,5},{5... | collective-permute-start | bytes 786440 | tf_op jit(solution)/shard_map/ppermute | solution.py:103
  354.9 9.2 %collective-permute-start.16 = (bf16[2,32,2048]{2,1,0:T(8,128)(2,1)S(1)}, bf16[2,32,2048]{2,1,0:T(8,128)(2,1)S(1)}, u32[]{:S(2)}, u32[]{:S(2)}) collective-permute-start(bf16[2,32,2048]{2,1,0:T(8,128)(2,1)S(1)} %slice_bitcast_fusion.4), channel_id=1, source_target_pairs={{0,2},{1,3},{2,0},{3,1},{4,6},{5,7},{6,4},{7,5},{8,10},{9,11},{10,... | collective-permute-start | bytes 786440 | tf_op jit(solution)/shard_map/ppermute | solution.py:108
  355.3 12.8 %collective-permute-start.29 = (bf16[2,32,2048]{2,1,0:T(8,128)(2,1)S(1)}, bf16[2,32,2048]{2,1,0:T(8,128)(2,1)S(1)}, u32[]{:S(2)}, u32[]{:S(2)}) collective-permute-start(bf16[2,32,2048]{2,1,0:T(8,128)(2,1)S(1)} %slice_bitcast_fusion), channel_id=1, source_target_pairs={{0,2},{1,3},{2,0},{3,1},{4,6},{5,7},{6,4},{7,5},{8,10},{9,11},{10,... | collective-permute-start | bytes 786440 | tf_op jit(solution)/shard_map/ppermute | solution.py:108
  360.1 8.0 %collective-permute-start.27 = (bf16[2,32,2048]{2,1,0:T(8,128)(2,1)S(1)}, bf16[2,32,2048]{2,1,0:T(8,128)(2,1)S(1)}, u32[]{:S(2)}, u32[]{:S(2)}) collective-permute-start(bf16[2,32,2048]{2,1,0:T(8,128)(2,1)S(1)} %slice_bitcast_fusion.2), channel_id=1, source_target_pairs={{0,4},{4,0},{8,12},{12,8},{16,20},{20,16},{24,28},{28,24},{1,5},{5... | collective-permute-start | bytes 786440 | tf_op jit(solution)/shard_map/ppermute | solution.py:103
  364.3 6.6 %collective-permute-start.17 = (bf16[64,2048]{1,0:T(8,128)(2,1)S(1)}, bf16[64,2048]{1,0:T(8,128)(2,1)S(1)}, u32[]{:S(2)}, u32[]{:S(2)}) collective-permute-start(bf16[64,2048]{1,0:T(8,128)(2,1)S(1)} %fusion.37), channel_id=1, source_target_pairs={{0,24},{4,28},{8,0},{12,4},{16,8},{20,12},{24,16},{28,20},{1,25},{... | collective-permute-start | bytes 786440 | tf_op jit(solution)/shard_map/ppermute | solution.py:93
  368.3 17.7 %collective-permute-start.30 = (bf16[64,2048]{1,0:T(8,128)(2,1)S(1)}, bf16[64,2048]{1,0:T(8,128)(2,1)S(1)}, u32[]{:S(2)}, u32[]{:S(2)}) collective-permute-start(bf16[64,2048]{1,0:T(8,128)(2,1)S(1)} %get-tuple-element.56), channel_id=1, source_target_pairs={{0,16},{4,20},{8,24},{12,28},{16,0},{20,4},{24,8},{28,12},{1,17},{... | collective-permute-start | bytes 786440 | tf_op jit(solution)/shard_map/ppermute | solution.py:93
  368.3 17.6 %collective-permute-start.31 = (bf16[64,2048]{1,0:T(8,128)(2,1)S(1)}, bf16[64,2048]{1,0:T(8,128)(2,1)S(1)}, u32[]{:S(2)}, u32[]{:S(2)}) collective-permute-start(bf16[64,2048]{1,0:T(8,128)(2,1)S(1)} %get-tuple-element.57), channel_id=1, source_target_pairs={{0,8},{4,12},{8,16},{12,20},{16,24},{20,28},{24,0},{28,4},{1,9},{5... | collective-permute-start | bytes 786440 | tf_op jit(solution)/shard_map/ppermute | solution.py:93
  (12 other events, 97.5 us)
